TPU v7x, 32 devices: a whole 2x2x4 slice. The times are simulated.
32 devices in a mesh: group: 2 (over y), expert: 8 (over z, core), dp: 2 (over x).
Axes of the slice: x: 2, y: 2, z: 4, core: 2. Of those that a mesh axis runs over, the one named last changes fastest.
Arguments:
- tokens: bfloat16 [2048, 7168], P(('group', 'expert'), 'dp'), parts along dimension 0, may hold values from -6 to 6
- expert_ids: int32 [2048, 8], P(('group', 'expert')), parts along dimension 0, may hold values from 0 to 15, all different within a row; in each aligned block of 128 rows (0 to 127, 128 to 255, ...) at most 96 rows name the same one
- route_weights: float32 [2048, 8], P(('group', 'expert')), parts along dimension 0, may hold values from 0.05 to 0.6
- w_gate: bfloat16 [16, 7168, 1024], P('expert', 'dp'), may hold values from -0.0625 to 0.0625
- w_up: bfloat16 [16, 7168, 1024], P('expert', 'dp'), may hold values from -0.0625 to 0.0625
- w_down: bfloat16 [16, 1024, 7168], P('expert', None, 'dp'), may hold values from -0.1875 to 0.1875
Outputs:
- combined: bfloat16 [2048, 7168], P(('group', 'expert'), 'dp'), parts along dimension 0
There are 2 independent parts, one for each index of `group`. A program takes and returns all parts, laid end to end along the dimension named above; an argument that names none is the same for every part. Nothing has to cross between parts.
Inputs may be any that keep to these rules, and one draw needn't show every extreme that they name: `expert_ids`: each row names 8 different experts. In each aligned block of 128 rows (the tokens of one index of expert) no expert is named by more than 96 rows, a bound that some block reaches in some or all blocks.
All inputs are finite; a program needn't handle non-finite values.
Results may differ from a plain program's by a relative error of at most 0.015.
Values may be sent and summed in bfloat16 or wider, within the bound.
No kernel may reach another device: no remote copies, remote signals or barrier semaphores. Data moves between devices by JAX's collectives and lax.ppermute only.
A program may use at most 192 MiB of HBM per device.

v0:
```python
import jax
import jax.numpy as jnp
from jax import lax
from jax.sharding import PartitionSpec as P

COPIES = 2


def choose_copies(totals, exp_dev, columns, copies):
    per_column = totals.reshape(columns, exp_dev)
    col_load = jnp.sum(per_column, axis=1)
    col_order = jnp.arange(columns, dtype=jnp.int32)
    _, heavy_cols = lax.top_k(col_load * columns + (columns - 1 - col_order), copies)
    _, light_cols = lax.top_k(col_order - col_load * columns, copies)
    local_order = jnp.arange(exp_dev, dtype=jnp.int32)
    heavy_rows = per_column[heavy_cols]
    _, best_local = lax.top_k(heavy_rows * exp_dev + (exp_dev - 1 - local_order)[None, :], 1)
    copied_ids = heavy_cols * exp_dev + best_local[:, 0]
    return (copied_ids, heavy_cols, light_cols)


def expert_capacity_list(token_column, selected_count, expert_table):
    slot_capacity = min(token_column * selected_count * 3 // (2 * expert_table), token_column // 2)
    popular_capacity = min(
        token_column, max(slot_capacity * 3 // 2, token_column * selected_count // expert_table)
    )
    return (slot_capacity, popular_capacity)


def per_device(tokens, expert_ids, route_weights, w_gate, w_up, w_down):
    columns = lax.axis_size("expert")
    column = lax.axis_index("expert")
    exp_dev = w_gate.shape[0]
    token_column, selected_count = expert_ids.shape
    feat_dev = tokens.shape[1]
    expert_table = exp_dev * columns
    slot_capacity, popular_capacity = expert_capacity_list(
        token_column, selected_count, expert_table
    )
    spare_rows = popular_capacity - slot_capacity
    slot_total = exp_dev * slot_capacity + spare_rows
    flat_ids = expert_ids.reshape(-1)
    onehot = (flat_ids[:, None] == jnp.arange(expert_table, dtype=jnp.int32)[None, :]).astype(
        jnp.int32
    )
    order_rank = jnp.sum((jnp.cumsum(onehot, axis=0) - 1) * onehot, axis=1)
    totals = lax.psum(jnp.sum(onehot, axis=0), "expert")
    copied_ids, heavy_cols, light_cols = choose_copies(totals, exp_dev, columns, COPIES)
    owned_here = heavy_cols == column
    local_pick = jnp.sum(jnp.where(owned_here, copied_ids % exp_dev, 0))
    spare_gate = w_gate[local_pick]
    spare_up = w_up[local_pick]
    spare_down = w_down[local_pick]
    copy_match = flat_ids[:, None] == copied_ids[None, :]
    in_main = order_rank < slot_capacity
    in_spare = (
        jnp.logical_not(in_main) & jnp.any(copy_match, axis=1) & (order_rank < popular_capacity)
    )
    spare_col = jnp.sum(jnp.where(copy_match, heavy_cols[None, :], 0), axis=1)
    target_col = jnp.where(in_main, flat_ids // exp_dev, spare_col)
    slot_index = jnp.where(
        in_main,
        flat_ids % exp_dev * slot_capacity + order_rank,
        exp_dev * slot_capacity + order_rank - slot_capacity,
    )
    kept_mask = in_main | in_spare
    position = jnp.where(kept_mask, target_col * slot_total + slot_index, columns * slot_total)
    token_of = jnp.arange(token_column * selected_count, dtype=jnp.int32) // selected_count
    slot_token = (
        jnp.full((columns * slot_total,), -1, jnp.int32).at[position].set(token_of, mode="drop")
    )
    filled = slot_token >= 0
    outgoing = jnp.where(
        filled[:, None], tokens[jnp.maximum(slot_token, 0)], jnp.zeros((), tokens.dtype)
    )
    received = lax.all_to_all(
        outgoing.reshape(columns, slot_total, feat_dev),
        "expert",
        split_axis=0,
        concat_axis=0,
        tiled=True,
    )
    main_in = received[:, : exp_dev * slot_capacity].reshape(
        columns, exp_dev, slot_capacity, feat_dev
    )
    spare_in = received[:, exp_dev * slot_capacity :][:, None]
    gate_main = jnp.einsum("necd,edf->necf", main_in, w_gate, preferred_element_type=jnp.float32)
    up_main = jnp.einsum("necd,edf->necf", main_in, w_up, preferred_element_type=jnp.float32)
    gate_spare = jnp.einsum(
        "nxsd,df->nxsf", spare_in, spare_gate, preferred_element_type=jnp.float32
    )
    up_spare = jnp.einsum("nxsd,df->nxsf", spare_in, spare_up, preferred_element_type=jnp.float32)
    hidden_parts = (
        lax.psum_scatter(
            gate_main.astype(jnp.bfloat16), "dp", scatter_dimension=3, tiled=True
        ).astype(jnp.float32),
        lax.psum_scatter(
            up_main.astype(jnp.bfloat16), "dp", scatter_dimension=3, tiled=True
        ).astype(jnp.float32),
        lax.psum_scatter(
            gate_spare.astype(jnp.bfloat16), "dp", scatter_dimension=3, tiled=True
        ).astype(jnp.float32),
        lax.psum_scatter(
            up_spare.astype(jnp.bfloat16), "dp", scatter_dimension=3, tiled=True
        ).astype(jnp.float32),
    )
    hidden_main = (jax.nn.silu(hidden_parts[0]) * hidden_parts[1]).astype(jnp.bfloat16)
    hidden_backup = (jax.nn.silu(hidden_parts[2]) * hidden_parts[3]).astype(jnp.bfloat16)
    main_next = jnp.einsum(
        "necf,efd->necd",
        lax.all_gather(hidden_main, "dp", axis=3, tiled=True),
        w_down,
        preferred_element_type=jnp.float32,
    )
    spare_next = jnp.einsum(
        "nxsf,fd->nxsd",
        lax.all_gather(hidden_backup, "dp", axis=3, tiled=True),
        spare_down,
        preferred_element_type=jnp.float32,
    )
    sent_back = jnp.concatenate(
        [
            main_next.astype(jnp.bfloat16).reshape(columns, exp_dev * slot_capacity, feat_dev),
            spare_next.astype(jnp.bfloat16).reshape(columns, spare_rows, feat_dev),
        ],
        axis=1,
    )
    returned = lax.all_to_all(sent_back, "expert", split_axis=0, concat_axis=0, tiled=True)
    flat_back = returned.reshape(columns * slot_total, feat_dev)
    picked = flat_back[jnp.minimum(position, columns * slot_total - 1)].astype(jnp.float32)
    scaled = (
        jnp.where(kept_mask, route_weights.reshape(-1), jnp.zeros((), jnp.float32))[:, None]
        * picked
    )
    return jnp.sum(scaled.reshape(token_column, selected_count, feat_dev), axis=1).astype(
        jnp.bfloat16
    )


def solution(mesh):
    in_specs = (
        P(("group", "expert"), "dp"),
        P(("group", "expert"), None),
        P(("group", "expert"), None),
        P("expert", "dp", None),
        P("expert", "dp", None),
        P("expert", None, "dp"),
    )
    out_specs = P(("group", "expert"), "dp")
    return jax.shard_map(
        per_device, mesh=mesh, in_specs=in_specs, out_specs=out_specs, check_vma=False
    )
```

profile of v0, /device:TPU:14, one launch (start us, length us, event | category | flops | bytes accessed | tf_op | source)
XLA Modules:
  0.0 665.0 jit_solution(12094353202070988197)
XLA Ops:
  7.7 4.5 reduce-window.6
  12.9 8.5 %psum.7 = s32[8,2]{1,0:T(8,128)S(1)} all-reduce(s32[8,2]{1,0:T(8,128)S(1)} %reshape.286), channel_id=1, replica_groups=mesh['group'=2,'expert'=8,'dp'=2] {'expert'}, use_global_device_ids=true, to_apply=%region_4.5 | all-reduce | flops 16 | bytes 128 | tf_op jit(solution)/shard_map/psum | solution.py:47
  24.6 4.3 scatter_custom_fusion
  29.1 7.9 %gather_fusion.1 = bf16[1280,3584]{1,0:T(8,128)(2,1)} fusion(bf16[128,3584]{1,0:T(8,128)(2,1)S(1)} %copy-done, s32[2048]{0:T(1024)S(1)} %pad_clamp_fusion), kind=kCustom, calls=%fused_computation.1 | custom fusion | bytes 18355200 | tf_op jit(solution)/shard_map/gather | solution.py:74
  37.0 7.8 %broadcast_select_fusion = bf16[8,160,3584]{2,1,0:T(8,128)(2,1)} fusion(bf16[8,160,3584]{2,1,0:T(8,128)(2,1)} %bitcast.88, pred[8,160]{1,0:T(8,128)(4,1)S(1)} %broadcast_in_dim.60), kind=kLoop, calls=%fused_computation.13 | loop fusion | flops 4587520 | bytes 18351360 | tf_op jit(solution)/shard_map/jit(_where)/select_n | solution.py:73
  44.8 203.6 %all_to_all.10 = bf16[8,160,3584]{2,1,0:T(8,128)(2,1)S(1)} all-to-all(bf16[8,160,3584]{2,1,0:T(8,128)(2,1)} %broadcast_select_fusion), channel_id=1, replica_groups=mesh['group'=2,'expert'=8,'dp'=2] {'expert'}, dimensions={0} | all-to-all | bytes 18350080 | tf_op jit(solution)/shard_map/all_to_all | solution.py:76
  248.4 3.7 slice.28
  254.2 14.2 %convert_bitcast_fusion = bf16[8,2,64,1024]{3,2,0,1:T(8,128)(2,1)} fusion(bf16[2,3584,1024]{2,1,0:T(8,128)(2,1)} %param.10, bf16[8,2,64,3584]{3,2,1,0:T(8,128)(2,1)} %bitcast.90), kind=kOutput, calls=%fused_computation.34 | convolution fusion | flops 7517241344 | bytes 24117248 | tf_op jit(solution)/shard_map/necd,edf->necf/dot_general | solution.py:88
  268.5 14.2 %convert_bitcast_fusion.1 = bf16[8,2,64,1024]{3,2,0,1:T(8,128)(2,1)} fusion(bf16[2,3584,1024]{2,1,0:T(8,128)(2,1)} %param.9, bf16[8,2,64,3584]{3,2,1,0:T(8,128)(2,1)} %bitcast.91), kind=kOutput, calls=%fused_computation.35 | convolution fusion | flops 7517241344 | bytes 24117248 | tf_op jit(solution)/shard_map/necd,edf->necf/dot_general | solution.py:87
  284.7 6.5 fusion.52
  291.3 6.6 fusion.57
  299.9 34.2 %reduce-scatter.5.cloned.1.call-done = bf16[8,2,64,512]{3,2,0,1:T(8,128)(2,1)} async-done(((bf16[8,2,64,1024]{3,2,0,1:T(8,128)(2,1)}), bf16[8,2,64,512]{3,2,0,1:T(8,128)(2,1)}) %reduce-scatter.5.cloned.1.call-update) | async-done | bytes 1048592 | tf_op jit(solution)/shard_map/reduce_scatter | solution.py:94
  337.3 13.6 %reduce-scatter.11.cloned.1.call-done = bf16[8,1,32,512]{3,2,0,1:T(8,128)(2,1)} async-done(((bf16[8,1,32,1024]{3,2,0,1:T(8,128)(2,1)}), bf16[8,1,32,512]{3,2,0,1:T(8,128)(2,1)}) %reduce-scatter.11.cloned.1.call-update) | async-done | bytes 262160 | tf_op jit(solution)/shard_map/reduce_scatter | solution.py:103
  350.9 16.8 %reduce-scatter.9.cloned.1.call-done = bf16[8,1,32,512]{3,2,0,1:T(8,128)(2,1)} async-done(((bf16[8,1,32,1024]{3,2,0,1:T(8,128)(2,1)}), bf16[8,1,32,512]{3,2,0,1:T(8,128)(2,1)}) %reduce-scatter.9.cloned.1.call-update) | async-done | bytes 262160 | tf_op jit(solution)/shard_map/reduce_scatter | solution.py:100
  368.9 8.7 %all_gather.7 = bf16[8,1,32,1024]{3,2,0,1:T(8,128)(2,1)S(1)} all-gather(bf16[8,1,32,512]{3,2,0,1:T(8,128)(2,1)S(1)} %fusion.67), channel_id=1, replica_groups=mesh['group'=2,'expert'=8,'dp'=2] {'dp'}, dimensions={3}, use_global_device_ids=true | all-gather | bytes 786432 | tf_op jit(solution)/shard_map/all_gather | solution.py:117
  377.6 5.6 fusion.24
  383.2 19.0 %all-gather.2.cloned.1.call-done = bf16[8,2,64,1024]{3,2,0,1:T(8,128)(2,1)} async-done(((bf16[8,2,64,512]{3,2,0,1:T(8,128)(2,1)}), bf16[8,2,64,1024]{3,2,0,1:T(8,128)(2,1)}) %all-gather.2.cloned.1.call-update) | async-done | bytes 2097168 | tf_op jit(solution)/shard_map/all_gather | solution.py:111
  402.2 13.5 %fusion.19 = bf16[8,2,64,3584]{3,2,0,1:T(8,128)(2,1)S(1)} fusion(bf16[8,2,64,1024]{3,2,0,1:T(8,128)(2,1)} %all-gather.2.cloned.1.call-done, bf16[2,1024,3584]{2,1,0:T(8,128)(2,1)} %param.11), kind=kOutput, calls=%fused_computation.24 | convolution fusion | flops 7519862784 | bytes 24117248 | tf_op jit(solution)/shard_map/necf,efd->necd/dot_general | solution.py:109
  415.7 3.6 copy.28
  419.3 6.9 %pad_maximum_fusion = bf16[8,160,3584]{2,1,0:T(8,128)(2,1)} fusion(bf16[8,32,3584]{2,1,0:T(8,128)(2,1)S(1)} %fusion.24, bf16[8,128,3584]{2,1,0:T(8,128)(2,1)} %bitcast.89), kind=kLoop, calls=%fused_computation.12 | loop fusion | flops 18350080 | bytes 18350080 | tf_op jit(solution)/shard_map/concatenate | solution.py:121
  426.3 5.6 all-to-all-start.1
  432.3 196.8 %all-to-all-done.1 = bf16[8,160,3584]{2,1,0:T(8,128)(2,1)} async-done(((bf16[8,160,3584]{2,1,0:T(8,128)(2,1)}), bf16[8,160,3584]{2,1,0:T(8,128)(2,1)}, u32[]{:S(2)}, u32[]{:S(2)}) %all-to-all-start.1) | async-done | bytes 9175072 | tf_op jit(solution)/shard_map/all_to_all | solution.py:128
  629.1 18.7 %gather_fusion.2 = bf16[1024,3584]{1,0:T(8,128)(2,1)} fusion(bf16[1280,3584]{1,0:T(8,128)(2,1)} %bitcast.27, s32[1024]{0:T(1024)S(1)} %broadcast_clamp_fusion), kind=kCustom, calls=%fused_computation.2 | custom fusion | bytes 14684160 | tf_op jit(solution)/shard_map/gather | solution.py:130
  647.8 10.7 %fusion = bf16[128,3584]{1,0:T(8,128)(2,1)} fusion(bf16[1024,3584]{1,0:T(8,128)(2,1)} %gather_fusion.2, f32[128,8]{1,0:T(8,128)S(1)} %or_select_fusion), kind=kLoop, calls=%fused_computation.5 | loop fusion | flops 10551296 | bytes 8261632 | tf_op jit(solution)/shard_map/reduce_sum | solution.py:135
  (63 shorter events, 14.2 us)
Async XLA Ops:
  6.5 22.5 %copy-start = (bf16[128,3584]{1,0:T(8,128)(2,1)S(1)}, bf16[128,3584]{1,0:T(8,128)(2,1)}, u32[]{:S(2)}) copy-start(bf16[128,3584]{1,0:T(8,128)(2,1)} %param.6) | copy-start | bytes 2752516
  6.5 293.4 %reduce-scatter.7.cloned.1.call-start = ((), (), s32[]{:S(2)}) async-start(), calls=%async_computation.7 | async-start | bytes 3145728 | tf_op jit(solution)/shard_map/reduce_scatter | solution.py:97
  248.4 5.7 copy-start.2
  268.4 65.6 %reduce-scatter.5.cloned.1.call-start = ((), (), s32[]{:S(2)}) async-start(), calls=%async_computation.6 | async-start | bytes 3145728 | tf_op jit(solution)/shard_map/reduce_scatter | solution.py:94
  282.7 68.2 %reduce-scatter.11.cloned.1.call-start = ((), (), s32[]{:S(2)}) async-start(), calls=%async_computation.10 | async-start | bytes 786432 | tf_op jit(solution)/shard_map/reduce_scatter | solution.py:103
  291.2 76.5 %reduce-scatter.9.cloned.1.call-start = ((), (), s32[]{:S(2)}) async-start(), calls=%async_computation.9 | async-start | bytes 786432 | tf_op jit(solution)/shard_map/reduce_scatter | solution.py:100
  297.9 104.4 %all-gather.2.cloned.1.call-start = ((), (), s32[]{:S(2)}) async-start(), calls=%async_computation.8 | async-start | bytes 3145728 | tf_op jit(solution)/shard_map/all_gather | solution.py:111
  426.3 5.7 copy-start.3
  426.3 202.8 %all-to-all-start.1 = ((bf16[8,160,3584]{2,1,0:T(8,128)(2,1)}), bf16[8,160,3584]{2,1,0:T(8,128)(2,1)}, u32[]{:S(2)}, u32[]{:S(2)}) async-start(bf16[8,160,3584]{2,1,0:T(8,128)(2,1)} %pad_maximum_fusion), calls=%async_computation.5 | async-start | bytes 18350080 | tf_op jit(solution)/shard_map/all_to_all | solution.py:128
  629.1 29.4 %copy-start.1 = (bf16[128,3584]{1,0:T(8,128)(2,1)S(1)}, bf16[128,3584]{1,0:T(8,128)(2,1)}, u32[]{:S(2)}) copy-start(bf16[128,3584]{1,0:T(8,128)(2,1)} %param.6) | copy-start | bytes 2752516
Sparse Core Ops, SparseCore 0:
  268.5 31.3 reduce-scatter.6
  302.2 31.8 reduce-scatter.4
  336.3 14.5 reduce-scatter.10
  353.1 14.5 reduce-scatter.8
  369.1 33.0 all-gather.1
where the time goes:
time: 671 us; the launch traced here: 665 us
  waiting for transfers between devices  282 us (42%)
  blocking collectives  221 us (33%)
  matrix products  60.6 us (9%)
  local copies, waits for them, and re-layouts  42.9 us (6%)
  other arithmetic  37.3 us (6%)
  between operations  15.3 us (2%)
    all_to_all x1, blocking collectives, per_device(): lax.all_to_all(outgoing.reshape(columns, slot_total, feat_dev), 'expert',...  204 us
    all_to_all x1, waiting for transfers between devices, per_device(): lax.all_to_all(sent_back, 'expert', split_axis=0, concat_axis=0, tiled=True)  197 us
    reduce_scatter x1, waiting for transfers between devices, per_device(): lax.psum_scatter(gate_main.astype(jnp.bfloat16), 'dp', scatter_dimension=...  34.2 us
    all_gather x1, waiting for transfers between devices, per_device(): lax.all_gather(hidden_main, 'dp', axis=3, tiled=True)  19 us
    gather x1, local copies, waits for them, and re-layouts, per_device(): flat_back[jnp.minimum(position, columns * slot_total - 1)]  18.7 us
    reduce_scatter x1, waiting for transfers between devices, per_device(): lax.psum_scatter(gate_spare.astype(jnp.bfloat16), 'dp', scatter_dimension...  16.8 us
    dot_general x1, matrix products, per_device(): jnp.einsum('necd,edf->necf', main_in, w_up, preferred_element_type=jnp.fl...  14.2 us
    dot_general x1, matrix products, per_device(): jnp.einsum('necd,edf->necf', main_in, w_gate, preferred_element_type=jnp....  14.2 us
  transfers between devices with their start and end apart: 6, of which 6 were waited for; matrix products, arithmetic and copies ran while one was open for 6% of the time, Pallas kernels for 0%

commit v1 on v0

v1 whole, which is shorter than its diff:
```python
import functools

import jax
import jax.numpy as jnp
from jax import lax
from jax.experimental import pallas as pl
from jax.experimental.pallas import tpu as pltpu
from jax.sharding import PartitionSpec as P

COPIES = 2
CORES = 2
LANES = 128
VMEM_LIMIT = 40 * 1024 * 1024


def capacities(token_column, selected_count, expert_table):
    slot_capacity = min(token_column * selected_count * 3 // (2 * expert_table), token_column // 2)
    popular_capacity = min(
        token_column, max(slot_capacity * 3 // 2, token_column * selected_count // expert_table)
    )
    return slot_capacity, popular_capacity


def round_up(value, unit):
    return -(-value // unit) * unit


def tile_of(size, most):
    return max(t for t in range(LANES, most + 1, LANES) if size % t == 0)


class Plan:
    def __init__(self, columns, exp_dev, token_column, selected_count, feat, hidden, parts):
        self.columns, self.exp_dev, self.tokens, self.topk = columns, exp_dev, token_column, selected_count
        self.feat, self.hidden, self.parts = feat, hidden, parts
        self.slot_cap, self.popular_cap = capacities(token_column, selected_count, columns * exp_dev)
        self.caps = [round_up(self.popular_cap, 16)] + [round_up(self.slot_cap, 16)] * (exp_dev - 1)
        self.starts = [CORES * sum(self.caps[:i]) for i in range(exp_dev)]
        self.rows = CORES * sum(self.caps)
        self.piece = hidden // parts

    def spans(self):
        for i, cap in enumerate(self.caps):
            for b in range(CORES):
                yield i, b, self.starts[i] + b * cap, cap


def local_of(i, first):
    return first if i == 0 else jnp.where(i - 1 < first, i - 1, i)


def route_kernel(pos_ref, info_ref, slot_ref, weight_ref, first_ref, *, plan):
    column = pos_ref[0]
    ids = info_ref[:, : plan.topk, :]
    weights = info_ref[:, plan.topk :, :]
    totals = [
        jnp.sum((ids == float(e)).astype(jnp.float32)) for e in range(plan.columns * plan.exp_dev)
    ]
    loads, best = [], []
    for c in range(plan.columns):
        own = totals[c * plan.exp_dev : (c + 1) * plan.exp_dev]
        load, top, where = own[0], own[0], jnp.int32(0)
        for i in range(1, plan.exp_dev):
            load = load + own[i]
            where = jnp.where(own[i] > top, i, where)
            top = jnp.maximum(own[i], top)
        loads.append(load)
        best.append(where)
    heavy_here = jnp.int32(0)
    for _ in range(COPIES):
        top, where = loads[0], jnp.int32(0)
        for c in range(1, plan.columns):
            where = jnp.where(loads[c] > top, c, where)
            top = jnp.maximum(loads[c], top)
        heavy_here = jnp.where(where == column, 1, heavy_here)
        loads = [jnp.where(where == c, -1.0, loads[c]) for c in range(plan.columns)]
    own_best = jnp.int32(0)
    for c in range(plan.columns):
        own_best = jnp.where(column == c, best[c], own_best)
    first = jnp.where(heavy_here == 1, own_best, 0)
    first_ref[0] = first
    earlier = (
        lax.broadcasted_iota(jnp.int32, (plan.tokens, plan.tokens), 0)
        < lax.broadcasted_iota(jnp.int32, (plan.tokens, plan.tokens), 1)
    ).astype(jnp.bfloat16)
    for i in range(plan.exp_dev):
        expert = (column * plan.exp_dev + local_of(i, first)).astype(jnp.float32)
        hit = ids == expert
        named = jnp.sum(hit.astype(jnp.float32), axis=1)
        weight_ref[i] = jnp.sum(jnp.where(hit, weights, 0.0), axis=1)
        rank = jnp.dot(named.astype(jnp.bfloat16), earlier, preferred_element_type=jnp.float32)
        cap = jnp.int32(plan.slot_cap)
        if i == 0:
            cap = jnp.where(heavy_here == 1, plan.popular_cap, cap)
        rank = rank.astype(jnp.int32)
        slot_ref[i] = jnp.where((named > 0.5) & (rank < cap), rank, -1)


def picks(slot_ref, i, block, cap):
    row = slot_ref[i, pl.ds(block, 1), :]
    return lax.broadcasted_iota(jnp.int32, (cap, row.shape[1]), 0) == row


def up_kernel(first_ref, pos_ref, slot_ref, mine_ref, other_ref, gate_ref, up_ref, out_ref, rows_ref, *, plan, at):
    @pl.when(pl.program_id(0) == 0)
    def _():
        step = tile_of(plan.feat, 512)
        for i, b, start, cap in plan.spans():
            select = picks(slot_ref, i, pos_ref[at + b], cap).astype(jnp.bfloat16)
            block_ref = (mine_ref, other_ref)[b]
            for k in range(0, plan.feat, step):
                rows_ref[start : start + cap, k : k + step] = jnp.dot(
                    select, block_ref[:, k : k + step], preferred_element_type=jnp.float32
                ).astype(jnp.bfloat16)

    first = first_ref[0]
    for i, cap in enumerate(plan.caps):
        local = local_of(i, first)
        span = slice(plan.starts[i], plan.starts[i] + CORES * cap)
        for half, weight_ref in enumerate((gate_ref, up_ref)):
            out_ref[half, span, :] = jnp.dot(
                rows_ref[span, :], weight_ref[local], preferred_element_type=jnp.float32
            ).astype(jnp.bfloat16)


def hidden_kernel(pos_ref, slot_ref, weight_ref, mine_ref, other_ref, out_ref, *, plan, at):
    for i, b, start, cap in plan.spans():
        block = pos_ref[at + b]
        chosen = picks(slot_ref, i, block, cap)
        scale = jnp.sum(jnp.where(chosen, weight_ref[i, pl.ds(block, 1), :], 0.0), axis=1, keepdims=True)
        span = slice(start, start + cap)
        gate = mine_ref[0, span, :].astype(jnp.float32) + other_ref[0, span, :].astype(jnp.float32)
        up = mine_ref[1, span, :].astype(jnp.float32) + other_ref[1, span, :].astype(jnp.float32)
        out_ref[span, :] = (gate / (1.0 + jnp.exp(-gate)) * up * scale).astype(jnp.bfloat16)


def down_kernel(first_ref, pos_ref, slot_ref, *refs, plan, at, part_at):
    pieces = refs[: plan.parts]
    down_ref, mine_ref, other_ref, dense_ref = refs[plan.parts :]

    @pl.when(pl.program_id(0) == 0)
    def _():
        first = first_ref[0]
        for i, b, start, cap in plan.spans():
            select = picks(slot_ref, i, pos_ref[at + b], cap).astype(jnp.bfloat16)
            for q, piece_ref in enumerate(pieces):
                offset = local_of(i, first) * plan.hidden + pos_ref[part_at + q] * plan.piece
                dense_ref[
                    b * plan.tokens : (b + 1) * plan.tokens,
                    pl.ds(pl.multiple_of(offset, LANES), plan.piece),
                ] = lax.dot_general(
                    select,
                    piece_ref[start : start + cap, :],
                    (((0,), (0,)), ((), ())),
                    preferred_element_type=jnp.float32,
                ).astype(jnp.bfloat16)

    weight = down_ref[...].reshape(plan.exp_dev * plan.hidden, down_ref.shape[2])
    total = jnp.dot(dense_ref[...], weight, preferred_element_type=jnp.float32)
    mine_ref[...] = total[: plan.tokens].astype(jnp.bfloat16)
    other_ref[...] = total[plan.tokens :].astype(jnp.bfloat16)


def whole(shape):
    return pl.BlockSpec(shape, lambda *_: (0,) * len(shape))


def call_route(plan, pos, info):
    lists = jax.ShapeDtypeStruct((plan.exp_dev, plan.columns, plan.tokens), jnp.int32)
    return pl.pallas_call(
        functools.partial(route_kernel, plan=plan),
        out_shape=(
            lists,
            jax.ShapeDtypeStruct(lists.shape, jnp.float32),
            jax.ShapeDtypeStruct((1,), jnp.int32),
        ),
        in_specs=[pl.BlockSpec(memory_space=pltpu.SMEM), pl.BlockSpec(memory_space=pltpu.VMEM)],
        out_specs=(
            pl.BlockSpec(memory_space=pltpu.VMEM),
            pl.BlockSpec(memory_space=pltpu.VMEM),
            pl.BlockSpec(memory_space=pltpu.SMEM),
        ),
        name="route",
    )(pos, info)


def call_up(plan, route, pos, mine, other, w_gate, w_up, at, part):
    slot, _, first = route
    units = plan.hidden if part is None else plan.piece
    tile = tile_of(plan.piece, 256)
    tiles = units // tile

    def weight_at(j, first_ref, pos_ref):
        return 0, 0, j if part is None else pos_ref[part] * tiles + j

    weight = pl.BlockSpec((plan.exp_dev, plan.feat, tile), weight_at)
    block = whole((plan.tokens, plan.feat))
    return pl.pallas_call(
        functools.partial(up_kernel, plan=plan, at=at),
        out_shape=jax.ShapeDtypeStruct((2, plan.rows, units), jnp.bfloat16),
        grid_spec=pltpu.PrefetchScalarGridSpec(
            num_scalar_prefetch=2,
            grid=(tiles,),
            in_specs=[whole(slot.shape), block, block, weight, weight],
            out_specs=pl.BlockSpec((2, plan.rows, tile), lambda j, *_: (0, 0, j)),
            scratch_shapes=[pltpu.VMEM((plan.rows, plan.feat), jnp.bfloat16)],
        ),
        compiler_params=pltpu.CompilerParams(vmem_limit_bytes=VMEM_LIMIT),
        cost_estimate=pl.CostEstimate(
            flops=4 * plan.rows * plan.feat * units,
            bytes_accessed=4 * plan.exp_dev * plan.feat * units,
            transcendentals=0,
        ),
        name="gate_up",
    )(first, pos, slot, mine, other, w_gate, w_up)


def call_hidden(plan, route, pos, mine, other, at):
    slot, weight, _ = route
    vmem = pl.BlockSpec(memory_space=pltpu.VMEM)
    return pl.pallas_call(
        functools.partial(hidden_kernel, plan=plan, at=at),
        out_shape=jax.ShapeDtypeStruct((plan.rows, plan.piece), jnp.bfloat16),
        in_specs=[pl.BlockSpec(memory_space=pltpu.SMEM)] + [vmem] * 4,
        out_specs=vmem,
        compiler_params=pltpu.CompilerParams(vmem_limit_bytes=VMEM_LIMIT),
        cost_estimate=pl.CostEstimate(
            flops=8 * plan.rows * plan.piece,
            bytes_accessed=10 * plan.rows * plan.piece,
            transcendentals=plan.rows * plan.piece,
        ),
        name="hidden",
    )(pos, slot, weight, mine, other)


def call_down(plan, route, pos, pieces, w_down, at, part_at):
    slot, _, first = route
    tile = tile_of(plan.feat, 512)
    out = jax.ShapeDtypeStruct((plan.tokens, plan.feat), jnp.bfloat16)
    out_block = pl.BlockSpec((plan.tokens, tile), lambda j, *_: (0, j))
    return pl.pallas_call(
        functools.partial(down_kernel, plan=plan, at=at, part_at=part_at),
        out_shape=(out, out),
        grid_spec=pltpu.PrefetchScalarGridSpec(
            num_scalar_prefetch=2,
            grid=(plan.feat // tile,),
            in_specs=[whole(slot.shape)]
            + [whole((plan.rows, plan.piece))] * plan.parts
            + [pl.BlockSpec((plan.exp_dev, plan.hidden, tile), lambda j, *_: (0, 0, j))],
            out_specs=(out_block, out_block),
            scratch_shapes=[
                pltpu.VMEM((CORES * plan.tokens, plan.exp_dev * plan.hidden), jnp.bfloat16)
            ],
        ),
        compiler_params=pltpu.CompilerParams(vmem_limit_bytes=VMEM_LIMIT),
        cost_estimate=pl.CostEstimate(
            flops=2 * CORES * plan.tokens * plan.exp_dev * plan.hidden * plan.feat,
            bytes_accessed=2 * plan.exp_dev * plan.hidden * plan.feat,
            transcendentals=0,
        ),
        name="down",
    )(first, pos, slot, *pieces, w_down)


def per_device(tokens, expert_ids, route_weights, w_gate, w_up, w_down):
    columns, parts = lax.axis_size("expert"), lax.axis_size("dp")
    chips = columns // CORES
    column, part = lax.axis_index("expert"), lax.axis_index("dp")
    chip, core = column // CORES, column % CORES
    plan = Plan(
        columns, w_gate.shape[0], *expert_ids.shape, tokens.shape[1], w_gate.shape[2], parts
    )

    def hop(x, pairs):
        return lax.ppermute(
            x, "expert", [(a * CORES + c, b * CORES + c) for a, b in pairs for c in range(CORES)]
        )

    def swap_cores(x):
        return lax.ppermute(x, "expert", [(i, i ^ 1) for i in range(columns)])

    info = jnp.concatenate([expert_ids.T.astype(jnp.float32), route_weights.T], axis=0)
    info = lax.all_gather(info, "expert", axis=0)

    arrived, source, back = [tokens], [chip], [None]
    if chips == 4:
        near = [(0, 1), (1, 0), (2, 3), (3, 2)]
        middle = [(1, 2), (2, 1)]
        outward = [(1, 0), (2, 3)]
        inner = (chip == 1) | (chip == 2)
        a1 = hop(tokens, near)
        a2 = hop(tokens, middle)
        b1 = hop(a1, middle)
        b2 = hop(a2, outward)
        c1 = hop(b1, outward)
        arrived += [a1, jnp.where(inner, a2, b2), jnp.where(inner, b1, c1)]
        source += [chip ^ 1, jnp.where(chip < 2, 2, 1), jnp.where(chip < 2, 3, 0)]
        back += [
            [near],
            [middle, [(0, 2), (3, 1)]],
            [[(0, 3), (3, 0)], [(1, 3), (2, 0)]],
        ]
    else:
        for s in range(1, chips):
            arrived.append(hop(tokens, [(z, (z + s) % chips) for z in range(chips)]))
            source.append((chip - s) % chips)
            back.append([[(z, (z - s) % chips) for z in range(chips)]])

    values = [column]
    for s in source:
        values += [s * CORES + core, s * CORES + 1 - core]
    part_at = len(values)
    values += [part, 1 - part] if parts == 2 else list(range(parts))
    pos = jnp.stack([jnp.asarray(v, jnp.int32) for v in values])

    route = call_route(plan, pos, info)
    total = []
    for s in range(chips):
        at = 1 + CORES * s
        mine = arrived[s]
        other = swap_cores(mine)
        if parts == 2:
            flip = [(0, 1), (1, 0)]
            away = call_up(plan, route, pos, mine, other, w_gate, w_up, at, part_at + 1)
            away = lax.ppermute(away, "dp", flip)
            here = call_up(plan, route, pos, mine, other, w_gate, w_up, at, part_at)
            hidden = call_hidden(plan, route, pos, here, away, at)
            pieces = [hidden, lax.ppermute(hidden, "dp", flip)]
        else:
            both = call_up(plan, route, pos, mine, other, w_gate, w_up, at, None)
            both = lax.psum_scatter(both, "dp", scatter_dimension=2, tiled=True)
            hidden = call_hidden(plan, route, pos, both, jnp.zeros_like(both), at)
            hidden = lax.all_gather(hidden, "dp", axis=0)
            pieces = [hidden[q] for q in range(parts)]
        kept, sent = call_down(plan, route, pos, pieces, w_down, at, part_at)
        summed = kept.astype(jnp.float32) + swap_cores(sent).astype(jnp.float32)
        if s == 0:
            total.append(summed)
        else:
            total += [hop(summed.astype(jnp.bfloat16), pairs) for pairs in back[s]]
    return sum(t.astype(jnp.float32) for t in total).astype(jnp.bfloat16)


def solution(mesh):
    in_specs = (
        P(("group", "expert"), "dp"),
        P(("group", "expert"), None),
        P(("group", "expert"), None),
        P("expert", "dp", None),
        P("expert", "dp", None),
        P("expert", None, "dp"),
    )
    out_specs = P(("group", "expert"), "dp")
    return jax.shard_map(
        per_device, mesh=mesh, in_specs=in_specs, out_specs=out_specs, check_vma=False
    )
```

time: 671 us -> 298 us (0.44)
  blocking collectives: 221 us -> 28.1 us
  waiting for transfers between devices: 282 us -> 109 us
  Pallas kernels: 0 us -> 114 us
  matrix products: 60.6 us -> 0 us
  local copies, waits for them, and re-layouts: 42.9 us -> 3.24 us
  other arithmetic: 37.3 us -> 6.38 us
  starting transfers between devices: 5.92 us -> 32.1 us
  between operations: 15.3 us -> 0.38 us
    all_to_all x1 -> x0, blocking collectives: 204 us -> none  [per_device(): lax.all_to_all(outgoing.reshape(columns, slot_total, feat_dev), 'expert',...]
    all_to_all x1 -> x0, waiting for transfers between devices: 197 us -> none  [per_device(): lax.all_to_all(sent_back, 'expert', split_axis=0, concat_axis=0, tiled=True)]
    pallas_call x0 -> x17, Pallas kernels: none -> 114 us  [the longest x8 63.8 us: call_up(): pl.pallas_call(functools.partial(up_kernel, plan=plan, at=at), out_shape=...]
    ppermute x0 -> x26, waiting for transfers between devices: none -> 109 us  [the longest x10 92.9 us: hop(): lax.ppermute(x, 'expert', [(a * CORES + c, b * CORES + c) for a, b in pai...]
    reduce_scatter x4 -> x0, waiting for transfers between devices: 66.4 us -> none  [the longest x1 34.2 us: per_device(): lax.psum_scatter(gate_main.astype(jnp.bfloat16), 'dp', scatter_dimension=...]
    dot_general x6 -> x0, matrix products: 60.6 us -> none  [the longest x1 14.2 us: per_device(): jnp.einsum('necd,edf->necf', main_in, w_up, preferred_element_type=jnp.fl...]
    ppermute x0 -> x26, starting transfers between devices: none -> 32.1 us  [the longest x10 22.8 us: hop(): lax.ppermute(x, 'expert', [(a * CORES + c, b * CORES + c) for a, b in pai...]
    gather x3 -> x0, local copies, waits for them, and re-layouts: 27.1 us -> none  [the longest x1 18.7 us: per_device(): flat_back[jnp.minimum(position, columns * slot_total - 1)]]
  transfers between devices with their start and end apart: 6 -> 26, of which waited for: 6 -> 7; matrix products, arithmetic and copies ran while one was open for 6% -> 2% of each run, Pallas kernels for 0% -> 39%
where the time goes in v1:
time: 298 us; the launch traced here: 293 us
  Pallas kernels  114 us (38%)
  waiting for transfers between devices  109 us (37%)
  starting transfers between devices  32.1 us (11%)
  blocking collectives  28.1 us (9%)
  other arithmetic  6.38 us (2%)
  local copies, waits for them, and re-layouts  3.24 us (1%)
    ppermute x10, waiting for transfers between devices, hop(): lax.ppermute(x, 'expert', [(a * CORES + c, b * CORES + c) for a, b in pai...  92.9 us
    pallas_call x8, Pallas kernels, call_up(): pl.pallas_call(functools.partial(up_kernel, plan=plan, at=at), out_shape=...  63.8 us
    pallas_call x4, Pallas kernels, call_down(): pl.pallas_call(functools.partial(down_kernel, plan=plan, at=at, part_at=p...  44.5 us
    all_gather x1, blocking collectives, per_device(): info = lax.all_gather(info, 'expert', axis=0)  28.1 us
    ppermute x10, starting transfers between devices, hop(): lax.ppermute(x, 'expert', [(a * CORES + c, b * CORES + c) for a, b in pai...  22.8 us
    ppermute x4, waiting for transfers between devices, per_device(): away = lax.ppermute(away, 'dp', flip)  8.44 us
    ppermute x4, waiting for transfers between devices, per_device(): pieces = [hidden, lax.ppermute(hidden, 'dp', flip)]  7.62 us
  transfers between devices with their start and end apart: 26, of which 7 were waited for; matrix products, arithmetic and copies ran while one was open for 2% of the time, Pallas kernels for 39%

profile of v1, /device:TPU:14, one launch (start us, length us, event | category | flops | bytes accessed | tf_op | source)
XLA Modules:
  0.0 292.8 jit_solution(10841246404785077962)
XLA Ops:
  0.5 4.6 %collective-permute-start.10 = (bf16[128,3584]{1,0:T(8,128)(2,1)}, bf16[128,3584]{1,0:T(8,128)(2,1)}, u32[]{:S(2)}, u32[]{:S(2)}) collective-permute-start(bf16[128,3584]{1,0:T(8,128)(2,1)} %mine_ref.3), channel_id=1, source_target_pairs={{4,8},{6,10},{8,4},{10,6},{5,9},{7,11},{9,5},{11,7},{20,24},{22,26... | collective-permute-start | bytes 2752520 | tf_op jit(solution)/shard_map/ppermute | solution.py:275
  5.1 17.2 %collective-permute-done.4.mine_ref = bf16[128,3584]{1,0:T(8,128)(2,1)S(1)} collective-permute-done((bf16[128,3584]{1,0:T(8,128)(2,1)}, bf16[128,3584]{1,0:T(8,128)(2,1)S(1)}, u32[]{:S(2)}, u32[]{:S(2)}) %collective-permute-start.4) | collective-permute-done | bytes 917536 | tf_op jit(solution)/shard_map/ppermute | solution.py:275
  22.3 3.5 %collective-permute-start.18 = (bf16[128,3584]{1,0:T(8,128)(2,1)S(1)}, bf16[128,3584]{1,0:T(8,128)(2,1)}, u32[]{:S(2)}, u32[]{:S(2)}) collective-permute-start(bf16[128,3584]{1,0:T(8,128)(2,1)S(1)} %collective-permute-done.4.mine_ref), channel_id=1, source_target_pairs={{4,8},{6,10},{8,4},{10,6},{5,9},{7,11},{9,5},{11,7},{20,24},{22,26... | collective-permute-start | bytes 2752520 | tf_op jit(solution)/shard_map/ppermute | solution.py:275
  30.1 28.1 %all-gather = f32[128,128]{1,0:T(8,128)} all-gather(f32[16,128]{1,0:T(8,128)S(1)} %pad_maximum_fusion), channel_id=2, replica_groups=mesh['group'=2,'expert'=8,'dp'=2] {'expert'}, dimensions={0}, use_global_device_ids=true | all-gather | bytes 73728 | tf_op jit(solution)/shard_map/all_gather | solution.py:283
  62.6 8.0 %gate_up.9 = bf16[2,320,512]{2,1,0:T(8,128)(2,1)S(1)} custom-call(s32[1]{0:T(128)} %get-tuple-element.16.first_ref, s32[11]{0:T(128)S(1)} %copy-done.3, s32[2,8,128]{2,1,0:T(8,128)S(1)} %copy-done.2, bf16[128,3584]{1,0:T(8,128)(2,1)S(1)} %copy-done, bf16[128,3584]{1,0:T(8,128)(2,1)S(1)} %collective-permute-done.other_ref, bf16[2,3584,1024]{2,1,0:T(8,128)(2,1)} %gate_ref.15, ...), custom_call_target="tpu_custom_call" | custom-call | flops 2348810240 | bytes 14680064 | tf_op jit(solution)/shard_map/gate_up/pallas_call | solution.py:198
  71.2 8.0 %gate_up.11 = bf16[2,320,512]{2,1,0:T(8,128)(2,1)S(1)} custom-call(s32[1]{0:T(128)} %get-tuple-element.16.first_ref, s32[11]{0:T(128)S(1)} %copy-done.3, s32[2,8,128]{2,1,0:T(8,128)S(1)} %copy-done.2, bf16[128,3584]{1,0:T(8,128)(2,1)S(1)} %collective-permute-done.4.mine_ref, bf16[128,3584]{1,0:T(8,128)(2,1)S(1)} %collective-permute-done.5.other_ref, ...), custom_call_target="tpu_custom_call" | custom-call | flops 2348810240 | bytes 14680064 | tf_op jit(solution)/shard_map/gate_up/pallas_call | solution.py:198
  80.7 3.1 %collective-permute-start.19 = (bf16[128,3584]{1,0:T(8,128)(2,1)}, bf16[128,3584]{1,0:T(8,128)(2,1)S(1)}, u32[]{:S(2)}, u32[]{:S(2)}) collective-permute-start(bf16[128,3584]{1,0:T(8,128)(2,1)} %collective-permute-done.18), channel_id=1, source_target_pairs={{4,0},{6,2},{8,12},{10,14},{5,1},{7,3},{9,13},{11,15},{20,16},{22,... | collective-permute-start | bytes 2752520 | tf_op jit(solution)/shard_map/ppermute | solution.py:275
  85.2 8.0 %gate_up.10.mine_ref = bf16[2,320,512]{2,1,0:T(8,128)(2,1)S(1)} custom-call(s32[1]{0:T(128)} %get-tuple-element.16.first_ref, s32[11]{0:T(128)S(1)} %copy-done.3, s32[2,8,128]{2,1,0:T(8,128)S(1)} %copy-done.2, bf16[128,3584]{1,0:T(8,128)(2,1)S(1)} %collective-permute-done.4.mine_ref, bf16[128,3584]{1,0:T(8,128)(2,1)S(1)} %collective-permute-done.5.other_ref, ...), custom_call_target="tpu_custom_call" | custom-call | flops 2348810240 | bytes 14680064 | tf_op jit(solution)/shard_map/gate_up/pallas_call | solution.py:198
  93.2 8.4 %collective-permute-done.6.other_ref = bf16[2,320,512]{2,1,0:T(8,128)(2,1)S(1)} collective-permute-done((bf16[2,320,512]{2,1,0:T(8,128)(2,1)S(1)}, bf16[2,320,512]{2,1,0:T(8,128)(2,1)S(1)}, u32[]{:S(2)}, u32[]{:S(2)}) %collective-permute-start.6) | collective-permute-done | bytes 655392 | tf_op jit(solution)/shard_map/ppermute | solution.py:325
  104.8 8.0 %gate_up.13 = bf16[2,320,512]{2,1,0:T(8,128)(2,1)S(1)} custom-call(s32[1]{0:T(128)} %get-tuple-element.16.first_ref, s32[11]{0:T(128)S(1)} %copy-done.3, s32[2,8,128]{2,1,0:T(8,128)S(1)} %copy-done.2, bf16[128,3584]{1,0:T(8,128)(2,1)S(1)} %broadcast_select_fusion.1.mine_ref, bf16[128,3584]{1,0:T(8,128)(2,1)S(1)} %collective-permute-done.12.other_ref, ...), custom_call_target="tpu_custom_call" | custom-call | flops 2348810240 | bytes 14680064 | tf_op jit(solution)/shard_map/gate_up/pallas_call | solution.py:198
  114.1 8.0 %gate_up.8.mine_ref = bf16[2,320,512]{2,1,0:T(8,128)(2,1)S(1)} custom-call(s32[1]{0:T(128)} %get-tuple-element.16.first_ref, s32[11]{0:T(128)S(1)} %copy-done.3, s32[2,8,128]{2,1,0:T(8,128)S(1)} %copy-done.2, bf16[128,3584]{1,0:T(8,128)(2,1)S(1)} %copy-done.1, bf16[128,3584]{1,0:T(8,128)(2,1)S(1)} %collective-permute-done.other_ref, ...), custom_call_target="tpu_custom_call" | custom-call | flops 2348810240 | bytes 14680064 | tf_op jit(solution)/shard_map/gate_up/pallas_call | solution.py:198
  123.9 8.0 %gate_up.12.mine_ref = bf16[2,320,512]{2,1,0:T(8,128)(2,1)S(1)} custom-call(s32[1]{0:T(128)} %get-tuple-element.16.first_ref, s32[11]{0:T(128)S(1)} %copy-done.3, s32[2,8,128]{2,1,0:T(8,128)S(1)} %copy-done.2, bf16[128,3584]{1,0:T(8,128)(2,1)S(1)} %broadcast_select_fusion.1.mine_ref, bf16[128,3584]{1,0:T(8,128)(2,1)S(1)} %collective-permute-done.12.other_ref, ...), custom_call_target="tpu_custom_call" | custom-call | flops 2348810240 | bytes 14680064 | tf_op jit(solution)/shard_map/gate_up/pallas_call | solution.py:198
  131.8 11.1 %down.5 = (bf16[128,3584]{1,0:T(8,128)(2,1)S(1)}, bf16[128,3584]{1,0:T(8,128)(2,1)S(1)}) custom-call(s32[1]{0:T(128)} %get-tuple-element.16.first_ref, s32[11]{0:T(128)S(1)} %copy-done.3, s32[2,8,128]{2,1,0:T(8,128)S(1)} %copy-done.2, bf16[320,512]{1,0:T(8,128)(2,1)S(1)} %hidden.5.refs_0_, bf16[320,512]{1,0:T(8,128)(2,1)S(1)} %collective-permute-done.7.refs_1_, ...), custom_call_target="tpu_custom_call" | custom-call | flops 3758096384 | bytes 14680064 | tf_op jit(solution)/shard_map/down/pallas_call | solution.py:241
  145.2 8.0 %gate_up.15 = bf16[2,320,512]{2,1,0:T(8,128)(2,1)S(1)} custom-call(s32[1]{0:T(128)} %get-tuple-element.16.first_ref, s32[11]{0:T(128)S(1)} %copy-done.3, s32[2,8,128]{2,1,0:T(8,128)S(1)} %copy-done.2, bf16[128,3584]{1,0:T(8,128)(2,1)S(1)} %broadcast_select_fusion.mine_ref, bf16[128,3584]{1,0:T(8,128)(2,1)S(1)} %collective-permute-done.20.other_ref, ...), custom_call_target="tpu_custom_call" | custom-call | flops 2348810240 | bytes 14680064 | tf_op jit(solution)/shard_map/gate_up/pallas_call | solution.py:198
  154.1 11.3 %down.4 = (bf16[128,3584]{1,0:T(8,128)(2,1)S(1)}, bf16[128,3584]{1,0:T(8,128)(2,1)S(1)}) custom-call(s32[1]{0:T(128)} %get-tuple-element.16.first_ref, s32[11]{0:T(128)S(1)} %copy-done.3, s32[2,8,128]{2,1,0:T(8,128)S(1)} %copy-done.2, bf16[320,512]{1,0:T(8,128)(2,1)S(1)} %hidden.4.refs_0_, bf16[320,512]{1,0:T(8,128)(2,1)S(1)} %collective-permute-done.2.refs_1_, ...), custom_call_target="tpu_custom_call" | custom-call | flops 3758096384 | bytes 14680064 | tf_op jit(solution)/shard_map/down/pallas_call | solution.py:241
  165.4 8.0 %gate_up.14.mine_ref = bf16[2,320,512]{2,1,0:T(8,128)(2,1)S(1)} custom-call(s32[1]{0:T(128)} %get-tuple-element.16.first_ref, s32[11]{0:T(128)S(1)} %copy-done.3, s32[2,8,128]{2,1,0:T(8,128)S(1)} %copy-done.2, bf16[128,3584]{1,0:T(8,128)(2,1)S(1)} %broadcast_select_fusion.mine_ref, bf16[128,3584]{1,0:T(8,128)(2,1)S(1)} %collective-permute-done.20.other_ref, ...), custom_call_target="tpu_custom_call" | custom-call | flops 2348810240 | bytes 14680064 | tf_op jit(solution)/shard_map/gate_up/pallas_call | solution.py:198
  173.4 11.1 %down.6 = (bf16[128,3584]{1,0:T(8,128)(2,1)S(1)}, bf16[128,3584]{1,0:T(8,128)(2,1)S(1)}) custom-call(s32[1]{0:T(128)} %get-tuple-element.16.first_ref, s32[11]{0:T(128)S(1)} %copy-done.3, s32[2,8,128]{2,1,0:T(8,128)S(1)} %copy-done.2, bf16[320,512]{1,0:T(8,128)(2,1)S(1)} %hidden.6.refs_0_, bf16[320,512]{1,0:T(8,128)(2,1)S(1)} %collective-permute-done.14.refs_1_, ...), custom_call_target="tpu_custom_call" | custom-call | flops 3758096384 | bytes 14680064 | tf_op jit(solution)/shard_map/down/pallas_call | solution.py:241
  188.1 7.6 %collective-permute-done.22.refs_1_ = bf16[320,512]{1,0:T(8,128)(2,1)S(1)} collective-permute-done((bf16[320,512]{1,0:T(8,128)(2,1)S(1)}, bf16[320,512]{1,0:T(8,128)(2,1)S(1)}, u32[]{:S(2)}, u32[]{:S(2)}) %collective-permute-start.22) | collective-permute-done | bytes 327712 | tf_op jit(solution)/shard_map/ppermute | solution.py:328
  195.7 11.1 %down.7 = (bf16[128,3584]{1,0:T(8,128)(2,1)S(1)}, bf16[128,3584]{1,0:T(8,128)(2,1)S(1)}) custom-call(s32[1]{0:T(128)} %get-tuple-element.16.first_ref, s32[11]{0:T(128)S(1)} %copy-done.3, s32[2,8,128]{2,1,0:T(8,128)S(1)} %copy-done.2, bf16[320,512]{1,0:T(8,128)(2,1)S(1)} %hidden.7.refs_0_, bf16[320,512]{1,0:T(8,128)(2,1)S(1)} %collective-permute-done.22.refs_1_, ...), custom_call_target="tpu_custom_call" | custom-call | flops 3758096384 | bytes 14680064 | tf_op jit(solution)/shard_map/down/pallas_call | solution.py:241
  208.4 3.8 %collective-permute-start.16 = (bf16[128,3584]{1,0:T(8,128)(2,1)S(1)}, bf16[128,3584]{1,0:T(8,128)(2,1)S(1)}, u32[]{:S(2)}, u32[]{:S(2)}) collective-permute-start(bf16[128,3584]{1,0:T(8,128)(2,1)S(1)} %add_convert_fusion.2), channel_id=1, source_target_pairs={{4,8},{6,10},{8,4},{10,6},{5,9},{7,11},{9,5},{11,7},{20,24},{22,26... | collective-permute-start | bytes 2752520 | tf_op jit(solution)/shard_map/ppermute | solution.py:275
  212.5 2.5 collective-permute-start.25
  215.7 17.5 %collective-permute-done.17 = bf16[128,3584]{1,0:T(8,128)(2,1)S(1)} collective-permute-done((bf16[128,3584]{1,0:T(8,128)(2,1)S(1)}, bf16[128,3584]{1,0:T(8,128)(2,1)S(1)}, u32[]{:S(2)}, u32[]{:S(2)}) %collective-permute-start.17) | collective-permute-done | bytes 917536 | tf_op jit(solution)/shard_map/ppermute | solution.py:275
  233.2 38.8 %collective-permute-done.16 = bf16[128,3584]{1,0:T(8,128)(2,1)S(1)} collective-permute-done((bf16[128,3584]{1,0:T(8,128)(2,1)S(1)}, bf16[128,3584]{1,0:T(8,128)(2,1)S(1)}, u32[]{:S(2)}, u32[]{:S(2)}) %collective-permute-start.16) | collective-permute-done | bytes 917536 | tf_op jit(solution)/shard_map/ppermute | solution.py:275
  272.0 19.1 %collective-permute-done.25 = bf16[128,3584]{1,0:T(8,128)(2,1)S(1)} collective-permute-done((bf16[128,3584]{1,0:T(8,128)(2,1)S(1)}, bf16[128,3584]{1,0:T(8,128)(2,1)S(1)}, u32[]{:S(2)}, u32[]{:S(2)}) %collective-permute-start.25) | collective-permute-done | bytes 917536 | tf_op jit(solution)/shard_map/ppermute | solution.py:275
  (65 shorter events, 29.9 us)
Async XLA Ops:
  0.0 22.3 %collective-permute-start.4 = (bf16[128,3584]{1,0:T(8,128)(2,1)}, bf16[128,3584]{1,0:T(8,128)(2,1)S(1)}, u32[]{:S(2)}, u32[]{:S(2)}) collective-permute-start(bf16[128,3584]{1,0:T(8,128)(2,1)} %mine_ref.3), channel_id=1, source_target_pairs={{0,4},{2,6},{4,0},{6,2},{8,12},{10,14},{12,8},{14,10},{1,5},{3,7},... | collective-permute-start | bytes 2752520 | tf_op jit(solution)/shard_map/ppermute | solution.py:275
  0.5 25.3 %collective-permute-start.10 = (bf16[128,3584]{1,0:T(8,128)(2,1)}, bf16[128,3584]{1,0:T(8,128)(2,1)}, u32[]{:S(2)}, u32[]{:S(2)}) collective-permute-start(bf16[128,3584]{1,0:T(8,128)(2,1)} %mine_ref.3), channel_id=1, source_target_pairs={{4,8},{6,10},{8,4},{10,6},{5,9},{7,11},{9,5},{11,7},{20,24},{22,26... | collective-permute-start | bytes 2752520 | tf_op jit(solution)/shard_map/ppermute | solution.py:275
  5.1 55.0 %collective-permute-start = (bf16[128,3584]{1,0:T(8,128)(2,1)}, bf16[128,3584]{1,0:T(8,128)(2,1)S(1)}, u32[]{:S(2)}, u32[]{:S(2)}) collective-permute-start(bf16[128,3584]{1,0:T(8,128)(2,1)} %mine_ref.3), channel_id=1, source_target_pairs={{0,2},{2,0},{4,6},{6,4},{8,10},{10,8},{12,14},{14,12},{1,3},{3,1},... | collective-permute-start | bytes 2752520 | tf_op jit(solution)/shard_map/ppermute | solution.py:280
  22.3 48.9 %collective-permute-start.5 = (bf16[128,3584]{1,0:T(8,128)(2,1)S(1)}, bf16[128,3584]{1,0:T(8,128)(2,1)S(1)}, u32[]{:S(2)}, u32[]{:S(2)}) collective-permute-start(bf16[128,3584]{1,0:T(8,128)(2,1)S(1)} %collective-permute-done.4.mine_ref), channel_id=1, source_target_pairs={{0,2},{2,0},{4,6},{6,4},{8,10},{10,8},{12,14},{14,12},{1,3},{3,1},... | collective-permute-start | bytes 2752520 | tf_op jit(solution)/shard_map/ppermute | solution.py:280
  22.3 58.4 %collective-permute-start.18 = (bf16[128,3584]{1,0:T(8,128)(2,1)S(1)}, bf16[128,3584]{1,0:T(8,128)(2,1)}, u32[]{:S(2)}, u32[]{:S(2)}) collective-permute-start(bf16[128,3584]{1,0:T(8,128)(2,1)S(1)} %collective-permute-done.4.mine_ref), channel_id=1, source_target_pairs={{4,8},{6,10},{8,4},{10,6},{5,9},{7,11},{9,5},{11,7},{20,24},{22,26... | collective-permute-start | bytes 2752520 | tf_op jit(solution)/shard_map/ppermute | solution.py:275
  25.8 58.0 %collective-permute-start.11 = (bf16[128,3584]{1,0:T(8,128)(2,1)}, bf16[128,3584]{1,0:T(8,128)(2,1)}, u32[]{:S(2)}, u32[]{:S(2)}) collective-permute-start(bf16[128,3584]{1,0:T(8,128)(2,1)} %collective-permute-done.10), channel_id=1, source_target_pairs={{4,0},{6,2},{8,12},{10,14},{5,1},{7,3},{9,13},{11,15},{20,16},{22,... | collective-permute-start | bytes 2752520 | tf_op jit(solution)/shard_map/ppermute | solution.py:275
  70.6 51.5 %collective-permute-start.1 = (bf16[2,320,512]{2,1,0:T(8,128)(2,1)S(1)}, bf16[2,320,512]{2,1,0:T(8,128)(2,1)S(1)}, u32[]{:S(2)}, u32[]{:S(2)}) collective-permute-start(bf16[2,320,512]{2,1,0:T(8,128)(2,1)S(1)} %gate_up.9), channel_id=1, source_target_pairs={{0,1},{1,0},{2,3},{3,2},{4,5},{5,4},{6,7},{7,6},{8,9},{9,8},{10,11... | collective-permute-start | bytes 1966088 | tf_op jit(solution)/shard_map/ppermute | solution.py:325
  79.1 22.5 %collective-permute-start.6 = (bf16[2,320,512]{2,1,0:T(8,128)(2,1)S(1)}, bf16[2,320,512]{2,1,0:T(8,128)(2,1)S(1)}, u32[]{:S(2)}, u32[]{:S(2)}) collective-permute-start(bf16[2,320,512]{2,1,0:T(8,128)(2,1)S(1)} %gate_up.11), channel_id=1, source_target_pairs={{0,1},{1,0},{2,3},{3,2},{4,5},{5,4},{6,7},{7,6},{8,9},{9,8},{10,11... | collective-permute-start | bytes 1966088 | tf_op jit(solution)/shard_map/ppermute | solution.py:325
  80.7 22.7 %collective-permute-start.19 = (bf16[128,3584]{1,0:T(8,128)(2,1)}, bf16[128,3584]{1,0:T(8,128)(2,1)S(1)}, u32[]{:S(2)}, u32[]{:S(2)}) collective-permute-start(bf16[128,3584]{1,0:T(8,128)(2,1)} %collective-permute-done.18), channel_id=1, source_target_pairs={{4,0},{6,2},{8,12},{10,14},{5,1},{7,3},{9,13},{11,15},{20,16},{22,... | collective-permute-start | bytes 2752520 | tf_op jit(solution)/shard_map/ppermute | solution.py:275
  85.1 19.7 %collective-permute-start.12 = (bf16[128,3584]{1,0:T(8,128)(2,1)S(1)}, bf16[128,3584]{1,0:T(8,128)(2,1)S(1)}, u32[]{:S(2)}, u32[]{:S(2)}) collective-permute-start(bf16[128,3584]{1,0:T(8,128)(2,1)S(1)} %broadcast_select_fusion.1.mine_ref), channel_id=1, source_target_pairs={{0,2},{2,0},{4,6},{6,4},{8,10},{10,8},{12,14},{14,12},{1,3},{3,1},... | collective-permute-start | bytes 2752520 | tf_op jit(solution)/shard_map/ppermute | solution.py:280
  102.5 29.3 %collective-permute-start.7 = (bf16[320,512]{1,0:T(8,128)(2,1)S(1)}, bf16[320,512]{1,0:T(8,128)(2,1)S(1)}, u32[]{:S(2)}, u32[]{:S(2)}) collective-permute-start(bf16[320,512]{1,0:T(8,128)(2,1)S(1)} %hidden.5.refs_0_), channel_id=1, source_target_pairs={{0,1},{1,0},{2,3},{3,2},{4,5},{5,4},{6,7},{7,6},{8,9},{9,8},{10,11... | collective-permute-start | bytes 983048 | tf_op jit(solution)/shard_map/ppermute | solution.py:328
  104.7 40.5 %collective-permute-start.20 = (bf16[128,3584]{1,0:T(8,128)(2,1)S(1)}, bf16[128,3584]{1,0:T(8,128)(2,1)S(1)}, u32[]{:S(2)}, u32[]{:S(2)}) collective-permute-start(bf16[128,3584]{1,0:T(8,128)(2,1)S(1)} %broadcast_select_fusion.mine_ref), channel_id=1, source_target_pairs={{0,2},{2,0},{4,6},{6,4},{8,10},{10,8},{12,14},{14,12},{1,3},{3,1},... | collective-permute-start | bytes 2752520 | tf_op jit(solution)/shard_map/ppermute | solution.py:280
  112.8 30.2 %collective-permute-start.13 = (bf16[2,320,512]{2,1,0:T(8,128)(2,1)S(1)}, bf16[2,320,512]{2,1,0:T(8,128)(2,1)S(1)}, u32[]{:S(2)}, u32[]{:S(2)}) collective-permute-start(bf16[2,320,512]{2,1,0:T(8,128)(2,1)S(1)} %gate_up.13), channel_id=1, source_target_pairs={{0,1},{1,0},{2,3},{3,2},{4,5},{5,4},{6,7},{7,6},{8,9},{9,8},{10,11... | collective-permute-start | bytes 1966088 | tf_op jit(solution)/shard_map/ppermute | solution.py:325
  123.0 31.1 %collective-permute-start.2 = (bf16[320,512]{1,0:T(8,128)(2,1)S(1)}, bf16[320,512]{1,0:T(8,128)(2,1)S(1)}, u32[]{:S(2)}, u32[]{:S(2)}) collective-permute-start(bf16[320,512]{1,0:T(8,128)(2,1)S(1)} %hidden.4.refs_0_), channel_id=1, source_target_pairs={{0,1},{1,0},{2,3},{3,2},{4,5},{5,4},{6,7},{7,6},{8,9},{9,8},{10,11... | collective-permute-start | bytes 983048 | tf_op jit(solution)/shard_map/ppermute | solution.py:328
  142.9 44.3 %collective-permute-start.8 = (bf16[128,3584]{1,0:T(8,128)(2,1)S(1)}, bf16[128,3584]{1,0:T(8,128)(2,1)S(1)}, u32[]{:S(2)}, u32[]{:S(2)}) collective-permute-start(bf16[128,3584]{1,0:T(8,128)(2,1)S(1)} %get-tuple-element.22), channel_id=1, source_target_pairs={{0,2},{2,0},{4,6},{6,4},{8,10},{10,8},{12,14},{14,12},{1,3},{3,1},... | collective-permute-start | bytes 2752520 | tf_op jit(solution)/shard_map/ppermute | solution.py:280
  143.9 29.5 %collective-permute-start.14 = (bf16[320,512]{1,0:T(8,128)(2,1)S(1)}, bf16[320,512]{1,0:T(8,128)(2,1)S(1)}, u32[]{:S(2)}, u32[]{:S(2)}) collective-permute-start(bf16[320,512]{1,0:T(8,128)(2,1)S(1)} %hidden.6.refs_0_), channel_id=1, source_target_pairs={{0,1},{1,0},{2,3},{3,2},{4,5},{5,4},{6,7},{7,6},{8,9},{9,8},{10,11... | collective-permute-start | bytes 983048 | tf_op jit(solution)/shard_map/ppermute | solution.py:328
  153.1 31.9 %collective-permute-start.21 = (bf16[2,320,512]{2,1,0:T(8,128)(2,1)S(1)}, bf16[2,320,512]{2,1,0:T(8,128)(2,1)S(1)}, u32[]{:S(2)}, u32[]{:S(2)}) collective-permute-start(bf16[2,320,512]{2,1,0:T(8,128)(2,1)S(1)} %gate_up.15), channel_id=1, source_target_pairs={{0,1},{1,0},{2,3},{3,2},{4,5},{5,4},{6,7},{7,6},{8,9},{9,8},{10,11... | collective-permute-start | bytes 1966088 | tf_op jit(solution)/shard_map/ppermute | solution.py:325
  165.4 49.6 %collective-permute-start.3 = (bf16[128,3584]{1,0:T(8,128)(2,1)S(1)}, bf16[128,3584]{1,0:T(8,128)(2,1)S(1)}, u32[]{:S(2)}, u32[]{:S(2)}) collective-permute-start(bf16[128,3584]{1,0:T(8,128)(2,1)S(1)} %get-tuple-element.20), channel_id=1, source_target_pairs={{0,2},{2,0},{4,6},{6,4},{8,10},{10,8},{12,14},{14,12},{1,3},{3,1},... | collective-permute-start | bytes 2752520 | tf_op jit(solution)/shard_map/ppermute | solution.py:280
  184.5 22.3 %collective-permute-start.15 = (bf16[128,3584]{1,0:T(8,128)(2,1)S(1)}, bf16[128,3584]{1,0:T(8,128)(2,1)S(1)}, u32[]{:S(2)}, u32[]{:S(2)}) collective-permute-start(bf16[128,3584]{1,0:T(8,128)(2,1)S(1)} %get-tuple-element.24), channel_id=1, source_target_pairs={{0,2},{2,0},{4,6},{6,4},{8,10},{10,8},{12,14},{14,12},{1,3},{3,1},... | collective-permute-start | bytes 2752520 | tf_op jit(solution)/shard_map/ppermute | solution.py:280
  187.4 28.3 %collective-permute-start.9 = (bf16[128,3584]{1,0:T(8,128)(2,1)S(1)}, bf16[128,3584]{1,0:T(8,128)(2,1)S(1)}, u32[]{:S(2)}, u32[]{:S(2)}) collective-permute-start(bf16[128,3584]{1,0:T(8,128)(2,1)S(1)} %add_convert_fusion.3), channel_id=1, source_target_pairs={{0,4},{2,6},{4,0},{6,2},{8,12},{10,14},{12,8},{14,10},{1,5},{3,7},... | collective-permute-start | bytes 2752520 | tf_op jit(solution)/shard_map/ppermute | solution.py:275
  207.1 26.0 %collective-permute-start.17 = (bf16[128,3584]{1,0:T(8,128)(2,1)S(1)}, bf16[128,3584]{1,0:T(8,128)(2,1)S(1)}, u32[]{:S(2)}, u32[]{:S(2)}) collective-permute-start(bf16[128,3584]{1,0:T(8,128)(2,1)S(1)} %add_convert_fusion.2), channel_id=1, source_target_pairs={{0,8},{2,10},{12,4},{14,6},{1,9},{3,11},{13,5},{15,7},{16,24},{18,... | collective-permute-start | bytes 2752520 | tf_op jit(solution)/shard_map/ppermute | solution.py:275
  208.4 63.6 %collective-permute-start.16 = (bf16[128,3584]{1,0:T(8,128)(2,1)S(1)}, bf16[128,3584]{1,0:T(8,128)(2,1)S(1)}, u32[]{:S(2)}, u32[]{:S(2)}) collective-permute-start(bf16[128,3584]{1,0:T(8,128)(2,1)S(1)} %add_convert_fusion.2), channel_id=1, source_target_pairs={{4,8},{6,10},{8,4},{10,6},{5,9},{7,11},{9,5},{11,7},{20,24},{22,26... | collective-permute-start | bytes 2752520 | tf_op jit(solution)/shard_map/ppermute | solution.py:275
  212.5 78.6 %collective-permute-start.25 = (bf16[128,3584]{1,0:T(8,128)(2,1)S(1)}, bf16[128,3584]{1,0:T(8,128)(2,1)S(1)}, u32[]{:S(2)}, u32[]{:S(2)}) collective-permute-start(bf16[128,3584]{1,0:T(8,128)(2,1)S(1)} %add_convert_fusion.1), channel_id=1, source_target_pairs={{4,12},{6,14},{8,0},{10,2},{5,13},{7,15},{9,1},{11,3},{20,28},{22,... | collective-permute-start | bytes 2752520 | tf_op jit(solution)/shard_map/ppermute | solution.py:275
  215.0 76.1 %collective-permute-start.24 = (bf16[128,3584]{1,0:T(8,128)(2,1)S(1)}, bf16[128,3584]{1,0:T(8,128)(2,1)S(1)}, u32[]{:S(2)}, u32[]{:S(2)}) collective-permute-start(bf16[128,3584]{1,0:T(8,128)(2,1)S(1)} %add_convert_fusion.1), channel_id=1, source_target_pairs={{0,12},{2,14},{12,0},{14,2},{1,13},{3,15},{13,1},{15,3},{16,28},{1... | collective-permute-start | bytes 2752520 | tf_op jit(solution)/shard_map/ppermute | solution.py:275
  (7 other events, 43.6 us)

commit v2 on v1

v2 whole, which is shorter than its diff:
```python
import functools

import jax
import jax.numpy as jnp
from jax import lax
from jax.experimental import pallas as pl
from jax.experimental.pallas import tpu as pltpu
from jax.sharding import PartitionSpec as P

COPIES = 2
CORES = 2
LANES = 128
VMEM_LIMIT = 4 * 1024 * 1024
UP_LIMIT = 9 * 1024 * 1024
DOWN_LIMIT = 12 * 1024 * 1024
BUFFERS = 2


def capacities(token_column, selected_count, expert_table):
    slot_capacity = min(token_column * selected_count * 3 // (2 * expert_table), token_column // 2)
    popular_capacity = min(
        token_column, max(slot_capacity * 3 // 2, token_column * selected_count // expert_table)
    )
    return slot_capacity, popular_capacity


def round_up(value, unit):
    return -(-value // unit) * unit


def tile_of(size, most):
    return max(t for t in range(LANES, most + 1, LANES) if size % t == 0)


class Plan:
    def __init__(self, columns, exp_dev, token_column, selected_count, feat, hidden, parts):
        self.columns, self.exp_dev, self.tokens, self.topk = columns, exp_dev, token_column, selected_count
        self.feat, self.hidden, self.parts = feat, hidden, parts
        self.slot_cap, self.popular_cap = capacities(token_column, selected_count, columns * exp_dev)
        self.caps = [round_up(self.popular_cap, 16)] + [round_up(self.slot_cap, 16)] * (exp_dev - 1)
        self.starts = [CORES * sum(self.caps[:i]) for i in range(exp_dev)]
        self.rows = CORES * sum(self.caps)
        self.piece = hidden // parts

    def spans(self):
        for i, cap in enumerate(self.caps):
            for b in range(CORES):
                yield i, b, self.starts[i] + b * cap, cap


def local_of(i, first):
    return first if i == 0 else jnp.where(i - 1 < first, i - 1, i)


def route_kernel(pos_ref, *refs, plan):
    slot_ref, weight_ref, first_ref = refs[-3:]
    column = pos_ref[0]
    info = jnp.concatenate([ref[...] for ref in refs[:-3]], axis=0)
    ids = info[:, : plan.topk, :]
    weights = info[:, plan.topk :, :]
    totals = [
        jnp.sum((ids == float(e)).astype(jnp.float32)) for e in range(plan.columns * plan.exp_dev)
    ]
    loads, best = [], []
    for c in range(plan.columns):
        own = totals[c * plan.exp_dev : (c + 1) * plan.exp_dev]
        load, top, where = own[0], own[0], jnp.int32(0)
        for i in range(1, plan.exp_dev):
            load = load + own[i]
            where = jnp.where(own[i] > top, i, where)
            top = jnp.maximum(own[i], top)
        loads.append(load)
        best.append(where)
    heavy_here = jnp.int32(0)
    for _ in range(COPIES):
        top, where = loads[0], jnp.int32(0)
        for c in range(1, plan.columns):
            where = jnp.where(loads[c] > top, c, where)
            top = jnp.maximum(loads[c], top)
        heavy_here = jnp.where(where == column, 1, heavy_here)
        loads = [jnp.where(where == c, -1.0, loads[c]) for c in range(plan.columns)]
    own_best = jnp.int32(0)
    for c in range(plan.columns):
        own_best = jnp.where(column == c, best[c], own_best)
    first = jnp.where(heavy_here == 1, own_best, 0)
    first_ref[0] = first
    earlier = (
        lax.broadcasted_iota(jnp.int32, (plan.tokens, plan.tokens), 0)
        < lax.broadcasted_iota(jnp.int32, (plan.tokens, plan.tokens), 1)
    ).astype(jnp.bfloat16)
    for i in range(plan.exp_dev):
        expert = (column * plan.exp_dev + local_of(i, first)).astype(jnp.float32)
        hit = ids == expert
        named = jnp.sum(hit.astype(jnp.float32), axis=1)
        weight_ref[i] = jnp.sum(jnp.where(hit, weights, 0.0), axis=1)
        rank = jnp.dot(named.astype(jnp.bfloat16), earlier, preferred_element_type=jnp.float32)
        cap = jnp.int32(plan.slot_cap)
        if i == 0:
            cap = jnp.where(heavy_here == 1, plan.popular_cap, cap)
        rank = rank.astype(jnp.int32)
        slot_ref[i] = jnp.where((named > 0.5) & (rank < cap), rank, -1)


def picks(slot_ref, i, block, cap):
    row = slot_ref[i, pl.ds(block, 1), :]
    return lax.broadcasted_iota(jnp.int32, (cap, row.shape[1]), 0) == row


def up_kernel(first_ref, pos_ref, slot_ref, mine_ref, other_ref, gate_ref, up_ref, out_ref, rows_ref, *, plan, at, part):
    step = tile_of(plan.feat, 512)
    for i, b, start, cap in plan.spans():
        select = picks(slot_ref, i, pos_ref[at + b], cap).astype(jnp.bfloat16)
        block_ref = (mine_ref, other_ref)[b]
        for k in range(0, plan.feat, step):
            rows_ref[start : start + cap, k : k + step] = jnp.dot(
                select, block_ref[:, k : k + step], preferred_element_type=jnp.float32
            ).astype(jnp.bfloat16)

    first = first_ref[0]
    for q in range(out_ref.shape[2] // plan.piece):
        units = pl.ds(pl.multiple_of((q if part is None else pos_ref[part]) * plan.piece, LANES), plan.piece)
        for i, cap in enumerate(plan.caps):
            local = local_of(i, first)
            span = slice(plan.starts[i], plan.starts[i] + CORES * cap)
            for half, weight_ref in enumerate((gate_ref, up_ref)):
                out_ref[half, span, q * plan.piece : (q + 1) * plan.piece] = jnp.dot(
                    rows_ref[span, :], weight_ref[local, :, units], preferred_element_type=jnp.float32
                ).astype(jnp.bfloat16)


def hidden_kernel(pos_ref, slot_ref, weight_ref, mine_ref, other_ref, out_ref, *, plan, at):
    for i, b, start, cap in plan.spans():
        block = pos_ref[at + b]
        chosen = picks(slot_ref, i, block, cap)
        scale = jnp.sum(jnp.where(chosen, weight_ref[i, pl.ds(block, 1), :], 0.0), axis=1, keepdims=True)
        span = slice(start, start + cap)
        gate = mine_ref[0, span, :].astype(jnp.float32) + other_ref[0, span, :].astype(jnp.float32)
        up = mine_ref[1, span, :].astype(jnp.float32) + other_ref[1, span, :].astype(jnp.float32)
        out_ref[span, :] = (gate / (1.0 + jnp.exp(-gate)) * up * scale).astype(jnp.bfloat16)


def down_kernel(first_ref, pos_ref, slot_ref, *refs, plan, at, part_at):
    pieces = refs[: plan.parts]
    down_ref, mine_ref, other_ref, dense_ref, tiles_ref, done = refs[plan.parts :]
    buffers, tile = tiles_ref.shape[0], tiles_ref.shape[3]
    copies = [
        pltpu.make_async_copy(
            down_ref.at[:, :, k * tile : (k + 1) * tile], tiles_ref.at[k % buffers], done.at[k]
        )
        for k in range(plan.feat // tile)
    ]
    for copy in copies[:buffers]:
        copy.start()
    first = first_ref[0]
    for i, b, start, cap in plan.spans():
        select = picks(slot_ref, i, pos_ref[at + b], cap).astype(jnp.bfloat16)
        for q, piece_ref in enumerate(pieces):
            offset = local_of(i, first) * plan.hidden + pos_ref[part_at + q] * plan.piece
            dense_ref[
                b * plan.tokens : (b + 1) * plan.tokens,
                pl.ds(pl.multiple_of(offset, LANES), plan.piece),
            ] = lax.dot_general(
                select,
                piece_ref[start : start + cap, :],
                (((0,), (0,)), ((), ())),
                preferred_element_type=jnp.float32,
            ).astype(jnp.bfloat16)

    for k, copy in enumerate(copies):
        copy.wait()
        weight = tiles_ref[k % buffers].reshape(plan.exp_dev * plan.hidden, tile)
        total = jnp.dot(dense_ref[...], weight, preferred_element_type=jnp.float32)
        span = slice(k * tile, (k + 1) * tile)
        mine_ref[:, span] = total[: plan.tokens].astype(jnp.bfloat16)
        other_ref[:, span] = total[plan.tokens :].astype(jnp.bfloat16)
        if k + buffers < len(copies):
            copies[k + buffers].start()


SMEM = pl.BlockSpec(memory_space=pltpu.SMEM)
VMEM = pl.BlockSpec(memory_space=pltpu.VMEM)
PARAMS = pltpu.CompilerParams(vmem_limit_bytes=VMEM_LIMIT)
COST = pl.CostEstimate(flops=1000, bytes_accessed=1000, transcendentals=0)


def after(x, *others):
    return lax.optimization_barrier((x, *others))[0]


class Order:
    def __init__(self, pos):
        self.pos = pos

    def follow(self, *results):
        self.pos = after(self.pos, *results)

    def run(self, call):
        result = call(self.pos)
        self.follow(*jax.tree.leaves(result))
        return result


def held(x):
    return pltpu.with_memory_space_constraint(x, pltpu.VMEM)


def call_route(plan, pos, infos):
    lists = jax.ShapeDtypeStruct((plan.exp_dev, plan.columns, plan.tokens), jnp.int32)
    return pl.pallas_call(
        functools.partial(route_kernel, plan=plan),
        out_shape=(
            lists,
            jax.ShapeDtypeStruct(lists.shape, jnp.float32),
            jax.ShapeDtypeStruct((1,), jnp.int32),
        ),
        in_specs=[SMEM] + [VMEM] * len(infos),
        out_specs=(VMEM, VMEM, SMEM),
        compiler_params=PARAMS,
        cost_estimate=COST,
        name="route",
    )(pos, *infos)


def call_up(plan, route, pos, mine, other, w_gate, w_up, at, part):
    slot, _, first = route
    return pl.pallas_call(
        functools.partial(up_kernel, plan=plan, at=at, part=part),
        out_shape=jax.ShapeDtypeStruct(
            (2, plan.rows, plan.hidden if part is None else plan.piece), jnp.bfloat16
        ),
        in_specs=[SMEM, SMEM] + [VMEM] * 5,
        out_specs=VMEM,
        scratch_shapes=[pltpu.VMEM((plan.rows, plan.feat), jnp.bfloat16)],
        compiler_params=pltpu.CompilerParams(vmem_limit_bytes=UP_LIMIT),
        cost_estimate=COST,
        name="gate_up",
    )(first, pos, slot, mine, other, held(w_gate), held(w_up))


def call_hidden(plan, route, pos, mine, other, at):
    slot, weight, _ = route
    return pl.pallas_call(
        functools.partial(hidden_kernel, plan=plan, at=at),
        out_shape=jax.ShapeDtypeStruct((plan.rows, plan.piece), jnp.bfloat16),
        in_specs=[SMEM] + [VMEM] * 4,
        out_specs=VMEM,
        compiler_params=PARAMS,
        cost_estimate=COST,
        name="hidden",
    )(pos, slot, weight, mine, other)


def call_down(plan, route, pos, pieces, w_down, at, part_at):
    slot, _, first = route
    tile = tile_of(plan.feat, 896)
    out = jax.ShapeDtypeStruct((plan.tokens, plan.feat), jnp.bfloat16)
    return pl.pallas_call(
        functools.partial(down_kernel, plan=plan, at=at, part_at=part_at),
        out_shape=(out, out),
        in_specs=[SMEM, SMEM] + [VMEM] * (1 + plan.parts) + [pl.BlockSpec(memory_space=pltpu.HBM)],
        out_specs=(VMEM, VMEM),
        scratch_shapes=[
            pltpu.VMEM((CORES * plan.tokens, plan.exp_dev * plan.hidden), jnp.bfloat16),
            pltpu.VMEM((BUFFERS, plan.exp_dev, plan.hidden, tile), jnp.bfloat16),
            pltpu.SemaphoreType.DMA((plan.feat // tile,)),
        ],
        compiler_params=pltpu.CompilerParams(vmem_limit_bytes=DOWN_LIMIT),
        cost_estimate=COST,
        name="down",
    )(first, pos, slot, *pieces, pltpu.with_memory_space_constraint(w_down, pltpu.HBM))


def per_device(tokens, expert_ids, route_weights, w_gate, w_up, w_down):
    columns, parts = lax.axis_size("expert"), lax.axis_size("dp")
    chips = columns // CORES
    column, part = lax.axis_index("expert"), lax.axis_index("dp")
    chip, core = column // CORES, column % CORES
    plan = Plan(
        columns, w_gate.shape[0], *expert_ids.shape, tokens.shape[1], w_gate.shape[2], parts
    )

    def hop(x, pairs):
        return lax.ppermute(
            x, "expert", [(a * CORES + c, b * CORES + c) for a, b in pairs for c in range(CORES)]
        )

    def swap_cores(x):
        return lax.ppermute(x, "expert", [(i, i ^ 1) for i in range(columns)])

    values, at = [column], []

    def list_blocks(source):
        away = (chip - source) % chips
        at.append(len(values))
        values.extend([away, chips + away])

    if chips == 4:
        sources = [chip, chip ^ 1, chip ^ 2, 3 - chip]
    else:
        sources = [(chip - s) % chips for s in range(chips)]
    for source in sources:
        list_blocks(source)
    part_at = len(values)
    values += [part, 1 - part] if parts == 2 else list(range(parts))
    pos = jnp.stack([jnp.asarray(v, jnp.int32) for v in values])

    def shift(s):
        return [(z, (z + s) % chips) for z in range(chips)]

    info = jnp.concatenate([expert_ids.T.astype(jnp.float32), route_weights.T], axis=0)
    info = [info] + [hop(info, shift(s)) for s in range(1, chips)]
    sent = after(tokens, *info[1:])
    info = jnp.stack(info)
    infos = [info, swap_cores(info)]

    inner = (chip == 1) | (chip == 2)
    near, middle, outward = [(0, 1), (1, 0), (2, 3), (3, 2)], [(1, 2), (2, 1)], [(1, 0), (2, 3)]
    if chips == 4:
        first, third = hop(sent, near), hop(sent, middle)
    else:
        first, *rest = [hop(sent, shift(s)) for s in range(1, chips)] or [None]

    flip = [(0, 1), (1, 0)]
    order = Order(pos)
    route = order.run(lambda pos: call_route(plan, pos, infos))

    def up(s, mine, other, which):
        piece = None if parts != 2 else part_at + which
        return order.run(lambda pos: call_up(plan, route, pos, mine, other, w_gate, w_up, at[s], piece))

    here, away, hidden, total = {}, {}, {}, {}

    def start(s, mine, other):
        if parts == 2:
            away[s] = lax.ppermute(up(s, mine, other, 1), "dp", flip)
        else:
            both = lax.psum_scatter(up(s, mine, other, 0), "dp", scatter_dimension=2, tiled=True)
            here[s], away[s] = both, jnp.zeros_like(both)

    def keep(s, mine, other):
        if parts == 2:
            here[s] = up(s, mine, other, 0)

    def join(s):
        own = order.run(lambda pos: call_hidden(plan, route, pos, here[s], away[s], at[s]))
        if parts == 2:
            hidden[s] = [own, lax.ppermute(own, "dp", flip)]
        else:
            own = lax.all_gather(own, "dp", axis=0)
            hidden[s] = [own[q] for q in range(parts)]

    def down(s):
        kept, shared = order.run(
            lambda pos: call_down(plan, route, pos, hidden[s], w_down, at[s], part_at)
        )
        total[s] = kept, swap_cores(shared)

    def send(s):
        summed = total[s][0].astype(jnp.float32) + total[s][1].astype(jnp.float32)
        relay = chips == 4 and s == 3
        if relay:
            (passed,) = total[2]
            summed += jnp.where(inner, passed, jnp.zeros_like(passed)).astype(jnp.float32)
            total[2] = (jnp.where(inner, jnp.zeros_like(passed), passed),)
        summed = summed.astype(jnp.bfloat16)
        order.follow(summed)
        if chips == 4:
            pairs = [near, [(0, 1), (1, 3), (2, 0), (3, 2)], [(0, 3), (1, 2), (2, 1), (3, 0)]][s - 1]
        else:
            pairs = shift(-s)
        total[s] = (hop(summed, pairs),)

    blocks = {0: [tokens, swap_cores(sent)]}

    def take(s, block):
        blocks[s] = [block, swap_cores(block)]

    def begin(s):
        start(s, *blocks[s])

    def go_on(s):
        keep(s, *blocks[s])

    begin(0)
    go_on(0)
    if chips == 4:
        first, third = after(first, order.pos), after(third, order.pos)
        take(1, first)
        relayed, other = hop(first, middle), hop(third, outward)
        join(0)
        begin(1)
        down(0)
        go_on(1)
        relayed = after(relayed, order.pos)
        take(2, jnp.where(inner, relayed, other))
        last = hop(relayed, outward)
        join(1)
        begin(2)
        down(1)
        go_on(2)
        join(2)
        send(1)
        take(3, jnp.where(inner, third, after(last, order.pos)))
        begin(3)
        down(2)
        go_on(3)
        join(3)
        order.follow(*total[1])
        send(2)
        down(3)
        send(3)
    else:
        join(0)
        down(0)
        for s in range(1, chips):
            take(s, [first, *rest][s - 1])
            begin(s)
            go_on(s)
            join(s)
            down(s)
            send(s)
    return sum(t.astype(jnp.float32) for s in range(chips) for t in total[s]).astype(jnp.bfloat16)


def solution(mesh):
    in_specs = (
        P(("group", "expert"), "dp"),
        P(("group", "expert"), None),
        P(("group", "expert"), None),
        P("expert", "dp", None),
        P("expert", "dp", None),
        P("expert", None, "dp"),
    )
    out_specs = P(("group", "expert"), "dp")
    return jax.shard_map(
        per_device, mesh=mesh, in_specs=in_specs, out_specs=out_specs, check_vma=False
    )
```

time: 298 us -> 241 us (0.81); the launches traced: 293 us -> 239 us
  blocking collectives: 28.1 us -> 0 us
  Pallas kernels: 114 us -> 90.2 us
  waiting for transfers between devices: 109 us -> 88.8 us
  local copies, waits for them, and re-layouts: 3.24 us -> 22 us
    ppermute x10 -> x11, waiting for transfers between devices: 92.9 us -> 50.6 us  [hop(): lax.ppermute(x, 'expert', [(a * CORES + c, b * CORES + c) for a, b in pai...]
    all_gather x1 -> x0, blocking collectives: 28.1 us -> none  [per_device(): info = lax.all_gather(info, 'expert', axis=0)]
    ppermute x8, waiting for transfers between devices: 16.1 us -> 36.2 us  [the longest x4 28.6 us: start(): away[s] = lax.ppermute(up(s, mine, other, 1), 'dp', flip)]
    unnamed x10 -> x18, local copies, waits for them, and re-layouts: 2.55 us -> 21.9 us
    pallas_call x8, Pallas kernels: 63.8 us -> 48.2 us  [call_up(): pl.pallas_call(functools.partial(up_kernel, plan=plan, at=at, part=part),...]
    pallas_call x4, Pallas kernels: 44.5 us -> 37.2 us  [call_down(): pl.pallas_call(functools.partial(down_kernel, plan=plan, at=at, part_at=p...]
    ppermute x10 -> x11, starting transfers between devices: 22.8 us -> 22.6 us  [hop(): lax.ppermute(x, 'expert', [(a * CORES + c, b * CORES + c) for a, b in pai...]
  transfers between devices with their start and end apart: 26 -> 28, of which waited for: 7 -> 11; matrix products, arithmetic and copies ran while one was open for 2% -> 1% of each run, Pallas kernels for 39% -> 34%
where the time goes in v2:
time: 241 us; the launch traced here: 239 us
  Pallas kernels  90.2 us (37%)
  waiting for transfers between devices  88.8 us (37%)
  starting transfers between devices  32.5 us (13%)
  local copies, waits for them, and re-layouts  22 us (9%)
  other arithmetic  5.15 us (2%)
    ppermute x11, waiting for transfers between devices, hop(): lax.ppermute(x, 'expert', [(a * CORES + c, b * CORES + c) for a, b in pai...  50.6 us
    pallas_call x8, Pallas kernels, call_up(): pl.pallas_call(functools.partial(up_kernel, plan=plan, at=at, part=part),...  48.2 us
    pallas_call x4, Pallas kernels, call_down(): pl.pallas_call(functools.partial(down_kernel, plan=plan, at=at, part_at=p...  37.2 us
    ppermute x4, waiting for transfers between devices, start(): away[s] = lax.ppermute(up(s, mine, other, 1), 'dp', flip)  28.6 us
    ppermute x11, starting transfers between devices, hop(): lax.ppermute(x, 'expert', [(a * CORES + c, b * CORES + c) for a, b in pai...  22.6 us
    unnamed x18, local copies, waits for them, and re-layouts  21.9 us
    ppermute x4, waiting for transfers between devices, join(): hidden[s] = [own, lax.ppermute(own, 'dp', flip)]  7.57 us
  transfers between devices with their start and end apart: 28, of which 11 were waited for; matrix products, arithmetic and copies ran while one was open for 1% of the time, Pallas kernels for 34%

profile of v2, /device:TPU:14, one launch (start us, length us, event | category | flops | bytes accessed | tf_op | source)
XLA Modules:
  0.0 239.3 jit_solution(14086911867083010687)
XLA Ops:
  9.9 4.8 %collective-permute-start.12 = (bf16[128,3584]{1,0:T(8,128)(2,1)}, bf16[128,3584]{1,0:T(8,128)(2,1)S(1)}, u32[]{:S(2)}, u32[]{:S(2)}) collective-permute-start(bf16[128,3584]{1,0:T(8,128)(2,1)} %mine_ref.3), channel_id=1, source_target_pairs={{4,8},{6,10},{8,4},{10,6},{5,9},{7,11},{9,5},{11,7},{20,24},{22,26... | collective-permute-start | bytes 2752520 | tf_op jit(solution)/shard_map/ppermute | solution.py:283
  17.3 5.2 %copy-done = bf16[2,3584,1024]{2,1,0:T(8,128)(2,1)S(1)} copy-done((bf16[2,3584,1024]{2,1,0:T(8,128)(2,1)S(1)}, bf16[2,3584,1024]{2,1,0:T(8,128)(2,1)}, u32[]{:S(2)}) %copy-start) | copy-done | bytes 14680088
  22.5 5.2 %copy-done.2 = bf16[2,3584,1024]{2,1,0:T(8,128)(2,1)S(1)} copy-done((bf16[2,3584,1024]{2,1,0:T(8,128)(2,1)S(1)}, bf16[2,3584,1024]{2,1,0:T(8,128)(2,1)}, u32[]{:S(2)}) %copy-start.2) | copy-done | bytes 14680088
  28.8 4.4 %gate_up.8 = bf16[2,320,512]{2,1,0:T(8,128)(2,1)S(1)} custom-call(s32[1]{0:T(128)} %get-tuple-element.40.first_ref, s32[11]{0:T(128)S(1)} %stack.56.pos_ref, s32[2,8,128]{2,1,0:T(8,128)S(1)} %get-tuple-element.41.slot_ref, bf16[128,3584]{1,0:T(8,128)(2,1)S(1)} %copy-done.4, bf16[128,3584]{1,0:T(8,128)(2,1)S(1)} %collective-permute-done.4.other_ref, ...), custom_call_target="tpu_custom_call" | custom-call | flops 1000 | bytes 1000 | tf_op jit(solution)/shard_map/gate_up/pallas_call | solution.py:226
  33.9 4.4 %gate_up.9.mine_ref = bf16[2,320,512]{2,1,0:T(8,128)(2,1)S(1)} custom-call(s32[1]{0:T(128)} %get-tuple-element.40.first_ref, s32[11]{0:T(128)S(1)} %stack.56.pos_ref, s32[2,8,128]{2,1,0:T(8,128)S(1)} %get-tuple-element.41.slot_ref, bf16[128,3584]{1,0:T(8,128)(2,1)S(1)} %copy-done.4, bf16[128,3584]{1,0:T(8,128)(2,1)S(1)} %collective-permute-done.4.other_ref, ...), custom_call_target="tpu_custom_call" | custom-call | flops 1000 | bytes 1000 | tf_op jit(solution)/shard_map/gate_up/pallas_call | solution.py:226
  42.9 7.1 %collective-permute-done.5.other_ref = bf16[2,320,512]{2,1,0:T(8,128)(2,1)S(1)} collective-permute-done((bf16[2,320,512]{2,1,0:T(8,128)(2,1)S(1)}, bf16[2,320,512]{2,1,0:T(8,128)(2,1)S(1)}, u32[]{:S(2)}, u32[]{:S(2)}) %collective-permute-start.5) | collective-permute-done | bytes 655392 | tf_op jit(solution)/shard_map/ppermute | solution.py:335
  51.6 5.2 %copy-done.1 = bf16[2,3584,1024]{2,1,0:T(8,128)(2,1)S(1)} copy-done((bf16[2,3584,1024]{2,1,0:T(8,128)(2,1)S(1)}, bf16[2,3584,1024]{2,1,0:T(8,128)(2,1)}, u32[]{:S(2)}) %copy-start.1) | copy-done | bytes 14680088
  56.8 5.2 %copy-done.3 = bf16[2,3584,1024]{2,1,0:T(8,128)(2,1)S(1)} copy-done((bf16[2,3584,1024]{2,1,0:T(8,128)(2,1)S(1)}, bf16[2,3584,1024]{2,1,0:T(8,128)(2,1)}, u32[]{:S(2)}) %copy-start.3) | copy-done | bytes 14680088
  62.0 4.5 %gate_up.10 = bf16[2,320,512]{2,1,0:T(8,128)(2,1)S(1)} custom-call(s32[1]{0:T(128)} %get-tuple-element.40.first_ref, s32[11]{0:T(128)S(1)} %stack.56.pos_ref, s32[2,8,128]{2,1,0:T(8,128)S(1)} %get-tuple-element.41.slot_ref, bf16[128,3584]{1,0:T(8,128)(2,1)S(1)} %collective-permute-done.6.mine_ref, bf16[128,3584]{1,0:T(8,128)(2,1)S(1)} %collective-permute-done.7.other_ref, ...), custom_call_target="tpu_custom_call" | custom-call | flops 1000 | bytes 1000 | tf_op jit(solution)/shard_map/gate_up/pallas_call | solution.py:226
  68.1 9.3 %down.4 = (bf16[128,3584]{1,0:T(8,128)(2,1)S(1)}, bf16[128,3584]{1,0:T(8,128)(2,1)S(1)}) custom-call(s32[1]{0:T(128)} %get-tuple-element.40.first_ref, s32[11]{0:T(128)S(1)} %stack.56.pos_ref, s32[2,8,128]{2,1,0:T(8,128)S(1)} %get-tuple-element.41.slot_ref, bf16[320,512]{1,0:T(8,128)(2,1)S(1)} %hidden.4.refs_0_, ...), custom_call_target="tpu_custom_call" | custom-call | flops 1000 | bytes 1000 | tf_op jit(solution)/shard_map/down/pallas_call | solution.py:257
  77.4 4.5 %gate_up.11.mine_ref = bf16[2,320,512]{2,1,0:T(8,128)(2,1)S(1)} custom-call(s32[1]{0:T(128)} %get-tuple-element.40.first_ref, s32[11]{0:T(128)S(1)} %stack.56.pos_ref, s32[2,8,128]{2,1,0:T(8,128)S(1)} %get-tuple-element.41.slot_ref, bf16[128,3584]{1,0:T(8,128)(2,1)S(1)} %collective-permute-done.6.mine_ref, ...), custom_call_target="tpu_custom_call" | custom-call | flops 1000 | bytes 1000 | tf_op jit(solution)/shard_map/gate_up/pallas_call | solution.py:226
  85.7 17.0 %gate_up.12 = bf16[2,320,512]{2,1,0:T(8,128)(2,1)S(1)} custom-call(s32[1]{0:T(128)} %get-tuple-element.40.first_ref, s32[11]{0:T(128)S(1)} %stack.56.pos_ref, s32[2,8,128]{2,1,0:T(8,128)S(1)} %get-tuple-element.41.slot_ref, bf16[128,3584]{1,0:T(8,128)(2,1)S(1)} %broadcast_select_fusion.1.mine_ref, bf16[128,3584]{1,0:T(8,128)(2,1)S(1)} %collective-permute-done.14.other_ref, ...), custom_call_target="tpu_custom_call" | custom-call | flops 1000 | bytes 1000 | tf_op jit(solution)/shard_map/gate_up/pallas_call | solution.py:226
  102.7 9.3 %down.5 = (bf16[128,3584]{1,0:T(8,128)(2,1)S(1)}, bf16[128,3584]{1,0:T(8,128)(2,1)S(1)}) custom-call(s32[1]{0:T(128)} %get-tuple-element.40.first_ref, s32[11]{0:T(128)S(1)} %stack.56.pos_ref, s32[2,8,128]{2,1,0:T(8,128)S(1)} %get-tuple-element.41.slot_ref, bf16[320,512]{1,0:T(8,128)(2,1)S(1)} %hidden.5.refs_0_, ...), custom_call_target="tpu_custom_call" | custom-call | flops 1000 | bytes 1000 | tf_op jit(solution)/shard_map/down/pallas_call | solution.py:257
  114.3 4.4 %gate_up.13.mine_ref = bf16[2,320,512]{2,1,0:T(8,128)(2,1)S(1)} custom-call(s32[1]{0:T(128)} %get-tuple-element.40.first_ref, s32[11]{0:T(128)S(1)} %stack.56.pos_ref, s32[2,8,128]{2,1,0:T(8,128)S(1)} %get-tuple-element.41.slot_ref, bf16[128,3584]{1,0:T(8,128)(2,1)S(1)} %broadcast_select_fusion.1.mine_ref, ...), custom_call_target="tpu_custom_call" | custom-call | flops 1000 | bytes 1000 | tf_op jit(solution)/shard_map/gate_up/pallas_call | solution.py:226
  118.7 10.5 %collective-permute-done.18.other_ref = bf16[2,320,512]{2,1,0:T(8,128)(2,1)S(1)} collective-permute-done((bf16[2,320,512]{2,1,0:T(8,128)(2,1)S(1)}, bf16[2,320,512]{2,1,0:T(8,128)(2,1)S(1)}, u32[]{:S(2)}, u32[]{:S(2)}) %collective-permute-start.18) | collective-permute-done | bytes 655392 | tf_op jit(solution)/shard_map/ppermute | solution.py:335
  130.3 4.2 %collective-permute-done.19 = bf16[128,3584]{1,0:T(8,128)(2,1)S(1)} collective-permute-done((bf16[128,3584]{1,0:T(8,128)(2,1)}, bf16[128,3584]{1,0:T(8,128)(2,1)S(1)}, u32[]{:S(2)}, u32[]{:S(2)}) %collective-permute-start.19) | collective-permute-done | bytes 917536 | tf_op jit(solution)/shard_map/ppermute | solution.py:283
  138.6 4.4 %gate_up.14 = bf16[2,320,512]{2,1,0:T(8,128)(2,1)S(1)} custom-call(s32[1]{0:T(128)} %get-tuple-element.40.first_ref, s32[11]{0:T(128)S(1)} %stack.56.pos_ref, s32[2,8,128]{2,1,0:T(8,128)S(1)} %get-tuple-element.41.slot_ref, bf16[128,3584]{1,0:T(8,128)(2,1)S(1)} %broadcast_select_fusion.mine_ref, bf16[128,3584]{1,0:T(8,128)(2,1)S(1)} %collective-permute-done.20.other_ref, ...), custom_call_target="tpu_custom_call" | custom-call | flops 1000 | bytes 1000 | tf_op jit(solution)/shard_map/gate_up/pallas_call | solution.py:226
  144.9 9.3 %down.6 = (bf16[128,3584]{1,0:T(8,128)(2,1)S(1)}, bf16[128,3584]{1,0:T(8,128)(2,1)S(1)}) custom-call(s32[1]{0:T(128)} %get-tuple-element.40.first_ref, s32[11]{0:T(128)S(1)} %stack.56.pos_ref, s32[2,8,128]{2,1,0:T(8,128)S(1)} %get-tuple-element.41.slot_ref, bf16[320,512]{1,0:T(8,128)(2,1)S(1)} %hidden.6.refs_0_, ...), custom_call_target="tpu_custom_call" | custom-call | flops 1000 | bytes 1000 | tf_op jit(solution)/shard_map/down/pallas_call | solution.py:257
  155.8 4.6 %gate_up.15.mine_ref = bf16[2,320,512]{2,1,0:T(8,128)(2,1)S(1)} custom-call(s32[1]{0:T(128)} %get-tuple-element.40.first_ref, s32[11]{0:T(128)S(1)} %stack.56.pos_ref, s32[2,8,128]{2,1,0:T(8,128)S(1)} %get-tuple-element.41.slot_ref, bf16[128,3584]{1,0:T(8,128)(2,1)S(1)} %broadcast_select_fusion.mine_ref, ...), custom_call_target="tpu_custom_call" | custom-call | flops 1000 | bytes 1000 | tf_op jit(solution)/shard_map/gate_up/pallas_call | solution.py:226
  160.4 11.0 %collective-permute-done.24.other_ref = bf16[2,320,512]{2,1,0:T(8,128)(2,1)S(1)} collective-permute-done((bf16[2,320,512]{2,1,0:T(8,128)(2,1)S(1)}, bf16[2,320,512]{2,1,0:T(8,128)(2,1)S(1)}, u32[]{:S(2)}, u32[]{:S(2)}) %collective-permute-start.24) | collective-permute-done | bytes 655392 | tf_op jit(solution)/shard_map/ppermute | solution.py:335
  176.0 5.7 %collective-permute-done.25.refs_1_ = bf16[320,512]{1,0:T(8,128)(2,1)S(1)} collective-permute-done((bf16[320,512]{1,0:T(8,128)(2,1)S(1)}, bf16[320,512]{1,0:T(8,128)(2,1)S(1)}, u32[]{:S(2)}, u32[]{:S(2)}) %collective-permute-start.25) | collective-permute-done | bytes 327712 | tf_op jit(solution)/shard_map/ppermute | solution.py:347
  181.6 9.3 %down.7 = (bf16[128,3584]{1,0:T(8,128)(2,1)S(1)}, bf16[128,3584]{1,0:T(8,128)(2,1)S(1)}) custom-call(s32[1]{0:T(128)} %get-tuple-element.40.first_ref, s32[11]{0:T(128)S(1)} %stack.56.pos_ref, s32[2,8,128]{2,1,0:T(8,128)S(1)} %get-tuple-element.41.slot_ref, bf16[320,512]{1,0:T(8,128)(2,1)S(1)} %hidden.7.refs_0_, ...), custom_call_target="tpu_custom_call" | custom-call | flops 1000 | bytes 1000 | tf_op jit(solution)/shard_map/down/pallas_call | solution.py:257
  191.5 4.8 %collective-permute-done.23 = bf16[128,3584]{1,0:T(8,128)(2,1)S(1)} collective-permute-done((bf16[128,3584]{1,0:T(8,128)(2,1)S(1)}, bf16[128,3584]{1,0:T(8,128)(2,1)S(1)}, u32[]{:S(2)}, u32[]{:S(2)}) %collective-permute-start.23) | collective-permute-done | bytes 917536 | tf_op jit(solution)/shard_map/ppermute | solution.py:283
  197.5 40.0 %collective-permute-done.27 = bf16[128,3584]{1,0:T(8,128)(2,1)S(1)} collective-permute-done((bf16[128,3584]{1,0:T(8,128)(2,1)S(1)}, bf16[128,3584]{1,0:T(8,128)(2,1)S(1)}, u32[]{:S(2)}, u32[]{:S(2)}) %collective-permute-start.27) | collective-permute-done | bytes 917536 | tf_op jit(solution)/shard_map/ppermute | solution.py:283
  (78 shorter events, 44.4 us)
Async XLA Ops:
  1.4 4.6 %collective-permute-start.1 = (f32[16,128]{1,0:T(8,128)S(1)}, f32[16,128]{1,0:T(8,128)S(1)}, u32[]{:S(2)}, u32[]{:S(2)}) collective-permute-start(f32[16,128]{1,0:T(8,128)S(1)} %get-tuple-element.76), channel_id=1, source_target_pairs={{0,8},{2,10},{4,12},{6,14},{8,0},{10,2},{12,4},{14,6},{1,9},{3,11}... | collective-permute-start | bytes 24584 | tf_op jit(solution)/shard_map/ppermute | solution.py:283
  7.6 9.7 %collective-permute-start.4 = (bf16[128,3584]{1,0:T(8,128)(2,1)}, bf16[128,3584]{1,0:T(8,128)(2,1)S(1)}, u32[]{:S(2)}, u32[]{:S(2)}) collective-permute-start(bf16[128,3584]{1,0:T(8,128)(2,1)} %mine_ref.3), channel_id=1, source_target_pairs={{0,2},{2,0},{4,6},{6,4},{8,10},{10,8},{12,14},{14,12},{1,3},{3,1},... | collective-permute-start | bytes 2752520 | tf_op jit(solution)/shard_map/ppermute | solution.py:288
  7.6 30.7 %collective-permute-start.6 = (bf16[128,3584]{1,0:T(8,128)(2,1)}, bf16[128,3584]{1,0:T(8,128)(2,1)S(1)}, u32[]{:S(2)}, u32[]{:S(2)}) collective-permute-start(bf16[128,3584]{1,0:T(8,128)(2,1)} %mine_ref.3), channel_id=1, source_target_pairs={{0,4},{2,6},{4,0},{6,2},{8,12},{10,14},{12,8},{14,10},{1,5},{3,7},... | collective-permute-start | bytes 2752520 | tf_op jit(solution)/shard_map/ppermute | solution.py:283
  9.9 30.5 %collective-permute-start.12 = (bf16[128,3584]{1,0:T(8,128)(2,1)}, bf16[128,3584]{1,0:T(8,128)(2,1)S(1)}, u32[]{:S(2)}, u32[]{:S(2)}) collective-permute-start(bf16[128,3584]{1,0:T(8,128)(2,1)} %mine_ref.3), channel_id=1, source_target_pairs={{4,8},{6,10},{8,4},{10,6},{5,9},{7,11},{9,5},{11,7},{20,24},{22,26... | collective-permute-start | bytes 2752520 | tf_op jit(solution)/shard_map/ppermute | solution.py:283
  33.2 16.9 %collective-permute-start.5 = (bf16[2,320,512]{2,1,0:T(8,128)(2,1)S(1)}, bf16[2,320,512]{2,1,0:T(8,128)(2,1)S(1)}, u32[]{:S(2)}, u32[]{:S(2)}) collective-permute-start(bf16[2,320,512]{2,1,0:T(8,128)(2,1)S(1)} %gate_up.8), channel_id=1, source_target_pairs={{0,1},{1,0},{2,3},{3,2},{4,5},{5,4},{6,7},{7,6},{8,9},{9,8},{10,11... | collective-permute-start | bytes 1966088 | tf_op jit(solution)/shard_map/ppermute | solution.py:335
  38.3 13.3 %collective-permute-start.7 = (bf16[128,3584]{1,0:T(8,128)(2,1)S(1)}, bf16[128,3584]{1,0:T(8,128)(2,1)S(1)}, u32[]{:S(2)}, u32[]{:S(2)}) collective-permute-start(bf16[128,3584]{1,0:T(8,128)(2,1)S(1)} %collective-permute-done.6.mine_ref), channel_id=1, source_target_pairs={{0,2},{2,0},{4,6},{6,4},{8,10},{10,8},{12,14},{14,12},{1,3},{3,1},... | collective-permute-start | bytes 2752520 | tf_op jit(solution)/shard_map/ppermute | solution.py:288
  38.4 43.5 %collective-permute-start.11 = (bf16[128,3584]{1,0:T(8,128)(2,1)S(1)}, bf16[128,3584]{1,0:T(8,128)(2,1)}, u32[]{:S(2)}, u32[]{:S(2)}) collective-permute-start(bf16[128,3584]{1,0:T(8,128)(2,1)S(1)} %collective-permute-done.6.mine_ref), channel_id=1, source_target_pairs={{4,8},{6,10},{8,4},{10,6},{5,9},{7,11},{9,5},{11,7},{20,24},{22,26... | collective-permute-start | bytes 2752520 | tf_op jit(solution)/shard_map/ppermute | solution.py:283
  40.4 41.5 %collective-permute-start.13 = (bf16[128,3584]{1,0:T(8,128)(2,1)S(1)}, bf16[128,3584]{1,0:T(8,128)(2,1)}, u32[]{:S(2)}, u32[]{:S(2)}) collective-permute-start(bf16[128,3584]{1,0:T(8,128)(2,1)S(1)} %collective-permute-done.12), channel_id=1, source_target_pairs={{4,0},{6,2},{8,12},{10,14},{5,1},{7,3},{9,13},{11,15},{20,16},{22,... | collective-permute-start | bytes 2752520 | tf_op jit(solution)/shard_map/ppermute | solution.py:283
  50.9 17.1 %collective-permute-start.8 = (bf16[320,512]{1,0:T(8,128)(2,1)S(1)}, bf16[320,512]{1,0:T(8,128)(2,1)S(1)}, u32[]{:S(2)}, u32[]{:S(2)}) collective-permute-start(bf16[320,512]{1,0:T(8,128)(2,1)S(1)} %hidden.4.refs_0_), channel_id=1, source_target_pairs={{0,1},{1,0},{2,3},{3,2},{4,5},{5,4},{6,7},{7,6},{8,9},{9,8},{10,11... | collective-permute-start | bytes 983048 | tf_op jit(solution)/shard_map/ppermute | solution.py:347
  66.5 16.8 %collective-permute-start.10 = (bf16[2,320,512]{2,1,0:T(8,128)(2,1)S(1)}, bf16[2,320,512]{2,1,0:T(8,128)(2,1)S(1)}, u32[]{:S(2)}, u32[]{:S(2)}) collective-permute-start(bf16[2,320,512]{2,1,0:T(8,128)(2,1)S(1)} %gate_up.10), channel_id=1, source_target_pairs={{0,1},{1,0},{2,3},{3,2},{4,5},{5,4},{6,7},{7,6},{8,9},{9,8},{10,11... | collective-permute-start | bytes 1966088 | tf_op jit(solution)/shard_map/ppermute | solution.py:335
  84.2 18.5 %collective-permute-start.15 = (bf16[320,512]{1,0:T(8,128)(2,1)S(1)}, bf16[320,512]{1,0:T(8,128)(2,1)S(1)}, u32[]{:S(2)}, u32[]{:S(2)}) collective-permute-start(bf16[320,512]{1,0:T(8,128)(2,1)S(1)} %hidden.5.refs_0_), channel_id=1, source_target_pairs={{0,1},{1,0},{2,3},{3,2},{4,5},{5,4},{6,7},{7,6},{8,9},{9,8},{10,11... | collective-permute-start | bytes 983048 | tf_op jit(solution)/shard_map/ppermute | solution.py:347
  112.0 18.1 %collective-permute-start.16 = (bf16[128,3584]{1,0:T(8,128)(2,1)S(1)}, bf16[128,3584]{1,0:T(8,128)(2,1)S(1)}, u32[]{:S(2)}, u32[]{:S(2)}) collective-permute-start(bf16[128,3584]{1,0:T(8,128)(2,1)S(1)} %get-tuple-element.59), channel_id=1, source_target_pairs={{0,2},{2,0},{4,6},{6,4},{8,10},{10,8},{12,14},{14,12},{1,3},{3,1},... | collective-permute-start | bytes 2752520 | tf_op jit(solution)/shard_map/ppermute | solution.py:288
  112.2 17.0 %collective-permute-start.18 = (bf16[2,320,512]{2,1,0:T(8,128)(2,1)S(1)}, bf16[2,320,512]{2,1,0:T(8,128)(2,1)S(1)}, u32[]{:S(2)}, u32[]{:S(2)}) collective-permute-start(bf16[2,320,512]{2,1,0:T(8,128)(2,1)S(1)} %gate_up.12), channel_id=1, source_target_pairs={{0,1},{1,0},{2,3},{3,2},{4,5},{5,4},{6,7},{7,6},{8,9},{9,8},{10,11... | collective-permute-start | bytes 1966088 | tf_op jit(solution)/shard_map/ppermute | solution.py:335
  112.9 21.6 %collective-permute-start.19 = (bf16[128,3584]{1,0:T(8,128)(2,1)}, bf16[128,3584]{1,0:T(8,128)(2,1)S(1)}, u32[]{:S(2)}, u32[]{:S(2)}) collective-permute-start(bf16[128,3584]{1,0:T(8,128)(2,1)} %collective-permute-done.11), channel_id=1, source_target_pairs={{4,0},{6,2},{8,12},{10,14},{5,1},{7,3},{9,13},{11,15},{20,16},{22,... | collective-permute-start | bytes 2752520 | tf_op jit(solution)/shard_map/ppermute | solution.py:283
  134.7 4.0 %collective-permute-start.20 = (bf16[128,3584]{1,0:T(8,128)(2,1)S(1)}, bf16[128,3584]{1,0:T(8,128)(2,1)S(1)}, u32[]{:S(2)}, u32[]{:S(2)}) collective-permute-start(bf16[128,3584]{1,0:T(8,128)(2,1)S(1)} %broadcast_select_fusion.mine_ref), channel_id=1, source_target_pairs={{0,2},{2,0},{4,6},{6,4},{8,10},{10,8},{12,14},{14,12},{1,3},{3,1},... | collective-permute-start | bytes 2752520 | tf_op jit(solution)/shard_map/ppermute | solution.py:288
  134.8 10.1 %collective-permute-start.21 = (bf16[320,512]{1,0:T(8,128)(2,1)S(1)}, bf16[320,512]{1,0:T(8,128)(2,1)S(1)}, u32[]{:S(2)}, u32[]{:S(2)}) collective-permute-start(bf16[320,512]{1,0:T(8,128)(2,1)S(1)} %hidden.6.refs_0_), channel_id=1, source_target_pairs={{0,1},{1,0},{2,3},{3,2},{4,5},{5,4},{6,7},{7,6},{8,9},{9,8},{10,11... | collective-permute-start | bytes 983048 | tf_op jit(solution)/shard_map/ppermute | solution.py:347
  136.2 37.5 %collective-permute-start.17 = (bf16[128,3584]{1,0:T(8,128)(2,1)S(1)}, bf16[128,3584]{1,0:T(8,128)(2,1)S(1)}, u32[]{:S(2)}, u32[]{:S(2)}) collective-permute-start(bf16[128,3584]{1,0:T(8,128)(2,1)S(1)} %add_convert_fusion.3), channel_id=1, source_target_pairs={{0,4},{2,6},{4,0},{6,2},{8,12},{10,14},{12,8},{14,10},{1,5},{3,7},... | collective-permute-start | bytes 2752520 | tf_op jit(solution)/shard_map/ppermute | solution.py:283
  154.2 19.6 %collective-permute-start.22 = (bf16[128,3584]{1,0:T(8,128)(2,1)S(1)}, bf16[128,3584]{1,0:T(8,128)(2,1)S(1)}, u32[]{:S(2)}, u32[]{:S(2)}) collective-permute-start(bf16[128,3584]{1,0:T(8,128)(2,1)S(1)} %get-tuple-element.67), channel_id=1, source_target_pairs={{0,2},{2,0},{4,6},{6,4},{8,10},{10,8},{12,14},{14,12},{1,3},{3,1},... | collective-permute-start | bytes 2752520 | tf_op jit(solution)/shard_map/ppermute | solution.py:288
  154.3 17.1 %collective-permute-start.24 = (bf16[2,320,512]{2,1,0:T(8,128)(2,1)S(1)}, bf16[2,320,512]{2,1,0:T(8,128)(2,1)S(1)}, u32[]{:S(2)}, u32[]{:S(2)}) collective-permute-start(bf16[2,320,512]{2,1,0:T(8,128)(2,1)S(1)} %gate_up.14), channel_id=1, source_target_pairs={{0,1},{1,0},{2,3},{3,2},{4,5},{5,4},{6,7},{7,6},{8,9},{9,8},{10,11... | collective-permute-start | bytes 1966088 | tf_op jit(solution)/shard_map/ppermute | solution.py:335
  172.3 9.3 %collective-permute-start.25 = (bf16[320,512]{1,0:T(8,128)(2,1)S(1)}, bf16[320,512]{1,0:T(8,128)(2,1)S(1)}, u32[]{:S(2)}, u32[]{:S(2)}) collective-permute-start(bf16[320,512]{1,0:T(8,128)(2,1)S(1)} %hidden.7.refs_0_), channel_id=1, source_target_pairs={{0,1},{1,0},{2,3},{3,2},{4,5},{5,4},{6,7},{7,6},{8,9},{9,8},{10,11... | collective-permute-start | bytes 983048 | tf_op jit(solution)/shard_map/ppermute | solution.py:347
  174.0 22.3 %collective-permute-start.23 = (bf16[128,3584]{1,0:T(8,128)(2,1)S(1)}, bf16[128,3584]{1,0:T(8,128)(2,1)S(1)}, u32[]{:S(2)}, u32[]{:S(2)}) collective-permute-start(bf16[128,3584]{1,0:T(8,128)(2,1)S(1)} %add_convert_fusion.2), channel_id=1, source_target_pairs={{0,4},{2,6},{4,12},{6,14},{8,0},{10,2},{12,8},{14,10},{1,5},{3,7},... | collective-permute-start | bytes 2752520 | tf_op jit(solution)/shard_map/ppermute | solution.py:283
  190.9 5.4 %collective-permute-start.26 = (bf16[128,3584]{1,0:T(8,128)(2,1)S(1)}, bf16[128,3584]{1,0:T(8,128)(2,1)S(1)}, u32[]{:S(2)}, u32[]{:S(2)}) collective-permute-start(bf16[128,3584]{1,0:T(8,128)(2,1)S(1)} %get-tuple-element.74), channel_id=1, source_target_pairs={{0,2},{2,0},{4,6},{6,4},{8,10},{10,8},{12,14},{14,12},{1,3},{3,1},... | collective-permute-start | bytes 2752520 | tf_op jit(solution)/shard_map/ppermute | solution.py:288
  191.0 6.5 %collective-permute-start.9 = (bf16[128,3584]{1,0:T(8,128)(2,1)S(1)}, bf16[128,3584]{1,0:T(8,128)(2,1)S(1)}, u32[]{:S(2)}, u32[]{:S(2)}) collective-permute-start(bf16[128,3584]{1,0:T(8,128)(2,1)S(1)} %get-tuple-element.51), channel_id=1, source_target_pairs={{0,2},{2,0},{4,6},{6,4},{8,10},{10,8},{12,14},{14,12},{1,3},{3,1},... | collective-permute-start | bytes 2752520 | tf_op jit(solution)/shard_map/ppermute | solution.py:288
  196.7 40.7 %collective-permute-start.27 = (bf16[128,3584]{1,0:T(8,128)(2,1)S(1)}, bf16[128,3584]{1,0:T(8,128)(2,1)S(1)}, u32[]{:S(2)}, u32[]{:S(2)}) collective-permute-start(bf16[128,3584]{1,0:T(8,128)(2,1)S(1)} %add_convert_fusion.1), channel_id=1, source_target_pairs={{0,12},{2,14},{4,8},{6,10},{8,4},{10,6},{12,0},{14,2},{1,13},{3,15... | collective-permute-start | bytes 2752520 | tf_op jit(solution)/shard_map/ppermute | solution.py:283
  (13 other events, 90.1 us)
